TPU v7x, 32 devices: a whole 2x2x4 slice. The times are simulated.
32 devices in a mesh: row: 8 (over y, x, core), col: 4 (over z).
Axes of the slice: x: 2, y: 2, z: 4, core: 2. Of those that a mesh axis runs over, the one named last changes fastest.
Arguments:
- queries: bfloat16 [1024, 2048], P('row', 'col'), may hold values from -48 to 48
- suffix_cache: bfloat16 [1024, 2048], P('row', 'col'), may hold values from -1.875 to 1.875
- suffix_leaf: int32 [8, 128], P('row'), may hold values from 0 to 31, never falling along the last dimension, each value on 1 to 8 neighbouring positions
- leaf_parent: int32 [8, 32], P('row'), may hold values from 0 to 7, as said below
- root_cache: bfloat16 [4096, 2048], P(('row', 'col')), may hold values from -2 to 2
- branch_cache: bfloat16 [8, 8192, 2048], P('row', 'col'), may hold values from -1.875 to 1.875
- branch_length: int32 [8], P('row'), may hold values from 1 to 8192, 49152 in all
- leaf_cache: bfloat16 [256, 256, 2048], P('row', 'col'), may hold values from -1.875 to 1.875
- leaf_length: int32 [256], P('row'), may hold values from 1 to 256, 32768 in all
Outputs:
- attention_out: bfloat16 [1024, 2048], P('row', 'col')
Inputs may be any that keep to these rules, and one draw needn't show every extreme that they name: `suffix_leaf`: never falls along a row's tokens; each of the 32 leaves has 1 to 8 tokens. `leaf_parent`: in each row index every branch node is the parent of exactly 4 of its leaves, so at most 32 of that row's tokens lie under one branch node.
All inputs are finite; a program needn't handle non-finite values. No bound on the sum of `branch_length` or of `leaf_length` on one device may be relied on, other than what follows from the above.
Results may differ from a plain program's by a relative error of at most 0.0065.
Values may be sent and summed in bfloat16 or wider, within the bound.
A program may use at most 128 MiB of HBM per device.

v0:
```python
import math

import jax
import jax.numpy as jnp
from jax import lax
from jax.sharding import PartitionSpec as P

HEADS = 8
KV_HEADS = 4
HEAD_DIM = 256
LEAF_ROW = 32


NEG = -1e30


def attend(queries, keys_values, usable):
    row_count = queries.shape[0]
    key_count = keys_values.shape[0]
    group_size = HEADS // KV_HEADS
    key_width = KV_HEADS * HEAD_DIM
    query_heads = queries.reshape(row_count, KV_HEADS, group_size, HEAD_DIM)
    key_heads = keys_values[:, :key_width].reshape(key_count, KV_HEADS, HEAD_DIM)
    value_heads = keys_values[:, key_width:].reshape(key_count, KV_HEADS, HEAD_DIM)
    scores = jnp.einsum(
        "rgjd,kgd->rgjk", query_heads, key_heads, preferred_element_type=jnp.float32
    ) * (1.0 / math.sqrt(HEAD_DIM))
    if usable is not None:
        key_mask = usable[:, None, None, :]
        scores = jnp.where(key_mask, scores, NEG)
    highest = jnp.max(scores, axis=-1)
    weights = jnp.exp(scores - highest[..., None])
    if usable is not None:
        weights = jnp.where(key_mask, weights, 0.0)
    totals = jnp.sum(weights, axis=-1)
    summed = jnp.einsum(
        "rgjk,kgd->rgjd",
        weights.astype(jnp.bfloat16),
        value_heads,
        preferred_element_type=jnp.float32,
    )
    return (
        highest.reshape(row_count, HEADS),
        totals.reshape(row_count, HEADS),
        summed.reshape(row_count, HEADS * HEAD_DIM),
    )


def merge_state(earlier, others):
    highest = jnp.maximum(earlier[0], others[0])
    keep_first = jnp.exp(earlier[0] - highest)
    keep_second = jnp.exp(others[0] - highest)
    totals = earlier[1] * keep_first + others[1] * keep_second
    summed = earlier[2] * jnp.repeat(keep_first, HEAD_DIM, axis=1) + others[2] * jnp.repeat(
        keep_second, HEAD_DIM, axis=1
    )
    return (highest, totals, summed)


def slice_heads(values, col_index, feature_width):
    per_slice = max(1, feature_width // HEAD_DIM)
    first_head = col_index * feature_width // HEAD_DIM
    chosen = lax.dynamic_slice_in_dim(values, first_head, per_slice, values.ndim - 1)
    return jnp.repeat(chosen, feature_width // per_slice, axis=values.ndim - 1)


def combine_columns(running):
    highest, totals, summed = running
    overall = lax.pmax(highest, "col")
    factors = jnp.exp(highest - overall)
    slice_sum = lax.psum_scatter(
        summed * jnp.repeat(factors, HEAD_DIM, axis=1), "col", scatter_dimension=1, tiled=True
    )
    overall_total = lax.psum(totals * factors, "col")
    return (overall, overall_total, slice_sum)


def on_device(
    queries,
    suffix_cache,
    suffix_leaf,
    leaf_parent,
    root_cache,
    branch_cache,
    branch_length,
    leaf_cache,
    leaf_length,
):
    col_count = lax.axis_size("col")
    row_count = lax.axis_size("row")
    col_index = lax.axis_index("col")
    full_queries, full_suffix = (
        lax.all_gather(queries, "col", axis=1, tiled=True),
        lax.all_gather(suffix_cache, "col", axis=1, tiled=True),
    )
    token_count = full_queries.shape[0]
    query_width = full_queries.shape[1]
    feature_width = queries.shape[1]
    leaf_local = suffix_leaf[0]
    positions = jnp.arange(token_count, dtype=jnp.int32)
    blank_state = (
        jnp.full((token_count, HEADS), NEG, jnp.float32),
        jnp.zeros((token_count, HEADS), jnp.float32),
        jnp.zeros((token_count, query_width), jnp.float32),
    )
    running = merge_state(
        blank_state,
        attend(full_queries, lax.all_gather(root_cache, "row", axis=0, tiled=True), None),
    )
    leaf_width = leaf_cache.shape[1]
    leaf_keys = leaf_cache.reshape(LEAF_ROW * leaf_width, leaf_cache.shape[2])
    key_slot = jnp.arange(LEAF_ROW * leaf_width, dtype=jnp.int32)
    key_leaf = key_slot // leaf_width
    key_place = col_index * leaf_width + key_slot % leaf_width
    leaf_ids = jnp.arange(LEAF_ROW, dtype=jnp.int32)
    key_live = jnp.any(
        (key_leaf[None, :] == leaf_ids[:, None]) & (key_place[None, :] < leaf_length[:, None]),
        axis=0,
    )
    usable = (leaf_local[:, None] == key_leaf[None, :]) & key_live[None, :]
    running = merge_state(running, attend(full_queries, leaf_keys, usable))
    suffix_width = token_count // col_count
    suffix_start = col_index * suffix_width
    suffix_keys = lax.dynamic_slice_in_dim(full_suffix, suffix_start, suffix_width, 0)
    suffix_owner = lax.dynamic_slice_in_dim(leaf_local, suffix_start, suffix_width, 0)
    suffix_place = suffix_start + jnp.arange(suffix_width, dtype=jnp.int32)
    usable = (leaf_local[:, None] == suffix_owner[None, :]) & (
        suffix_place[None, :] <= positions[:, None]
    )
    running = merge_state(running, attend(full_queries, suffix_keys, usable))
    parents = leaf_parent[0]
    token_node = jnp.sum(
        jnp.where(leaf_local[:, None] == leaf_ids[None, :], parents[None, :], 0), axis=1
    )
    node_ids = jnp.arange(row_count, dtype=jnp.int32)
    node_hits = (token_node[:, None] == node_ids[None, :]).astype(jnp.int32)
    rank_in_node = jnp.sum(node_hits * (jnp.cumsum(node_hits, axis=0) - 1), axis=1)
    capacity = token_count // 16 * (LEAF_ROW // row_count)
    slot_index = token_node * capacity + rank_in_node
    slot_token = (
        jnp.full((row_count * capacity,), token_count, jnp.int32).at[slot_index].set(positions)
    )
    padded = jnp.concatenate(
        [full_queries, jnp.zeros((1, query_width), full_queries.dtype)], axis=0
    )
    outgoing = padded[slot_token].reshape(row_count, capacity, query_width)
    branch_keys = branch_cache[0]
    branch_width = branch_keys.shape[0]
    branch_place = col_index * branch_width + jnp.arange(branch_width, dtype=jnp.int32)
    branch_usable = (branch_place < branch_length[0])[None, :]
    arrived = lax.all_to_all(outgoing, "row", split_axis=0, concat_axis=0, tiled=True)
    sources = arrived.shape[0]
    item_count = arrived.shape[1]
    flat_queries = arrived.reshape(sources * item_count, arrived.shape[2])
    highest, totals, summed = attend(flat_queries, branch_keys, branch_usable)
    returned = (
        lax.all_to_all(
            summed.reshape(sources, item_count, query_width),
            "row",
            split_axis=0,
            concat_axis=0,
            tiled=True,
        ),
        lax.all_to_all(
            highest.reshape(sources, item_count, HEADS),
            "row",
            split_axis=0,
            concat_axis=0,
            tiled=True,
        ),
        lax.all_to_all(
            totals.reshape(sources, item_count, HEADS),
            "row",
            split_axis=0,
            concat_axis=0,
            tiled=True,
        ),
    )
    back_sums = returned[0].reshape(row_count * capacity, returned[0].shape[2])[slot_index]
    back_peaks = returned[1].reshape(row_count * capacity, HEADS)[slot_index]
    back_totals = returned[2].reshape(row_count * capacity, HEADS)[slot_index]
    running = merge_state(running, (back_peaks, back_totals, back_sums))
    highest, totals, summed = combine_columns(running)
    output = summed / slice_heads(totals, col_index, feature_width)
    return output.astype(jnp.bfloat16)


def solution(mesh):
    in_specs = (
        P("row", "col"),
        P("row", "col"),
        P("row", None),
        P("row", None),
        P(("row", "col"), None),
        P("row", "col", None),
        P("row"),
        P("row", "col", None),
        P("row"),
    )
    out_specs = P("row", "col")
    return jax.shard_map(
        on_device, mesh=mesh, in_specs=in_specs, out_specs=out_specs, check_vma=False
    )
```

profile of v0, /device:TPU:0, one launch (start us, length us, event | category | flops | bytes accessed | tf_op | source)
XLA Modules:
  0.0 235.4 jit_solution(15354557494574238933)
XLA Ops:
  6.5 0.8 select_reduce_fusion.1
  7.8 1.0 scatter_custom_fusion
  8.8 17.6 %all_gather.10 = bf16[128,2048]{1,0:T(8,128)(2,1)S(1)} all-gather(bf16[128,512]{1,0:T(8,128)(2,1)} %param.9), channel_id=1, replica_groups=mesh['row'=8,'col'=4] {'col'}, dimensions={1}, use_global_device_ids=true | all-gather | bytes 655360 | tf_op jit(solution)/shard_map/all_gather | solution.py:93
  26.4 2.3 gather_fusion
  28.7 4.4 %all-to-all-start = ((bf16[8,32,2048]{2,1,0:T(8,128)(2,1)}), bf16[8,32,2048]{2,1,0:T(8,128)(2,1)}, u32[]{:S(2)}, u32[]{:S(2)}) async-start(bf16[8,32,2048]{2,1,0:T(8,128)(2,1)} %bitcast.30), calls=%async_computation | async-start | bytes 2097152 | tf_op jit(solution)/shard_map/all_to_all | solution.py:151
  33.2 1.0 copy.201
  35.4 1.5 compare_and_fusion
  36.9 16.8 %all_gather.11 = bf16[128,2048]{1,0:T(8,128)(2,1)S(1)} all-gather(bf16[128,512]{1,0:T(8,128)(2,1)S(1)} %copy-done.4), channel_id=1, replica_groups=mesh['row'=8,'col'=4] {'col'}, dimensions={1}, use_global_device_ids=true | all-gather | bytes 655360 | tf_op jit(solution)/shard_map/all_gather | solution.py:94
  53.8 12.4 %copy.227 = bf16[1,2048,2048]{1,2,0:T(8,128)(2,1)} copy(bf16[1,2048,2048]{2,1,0:T(8,128)(2,1)} %param.14) | data formatting | bytes 16777216 | tf_op args[5]
  66.2 6.1 %fusion.80 = (bf16[2048,1024]{0,1:T(8,128)(2,1)}, bf16[2048,1024]{0,1:T(8,128)(2,1)}) fusion(bf16[2048,2048]{0,1:T(8,128)(2,1)} %bitcast.152), kind=kLoop, calls=%fused_computation.115 | loop fusion | bytes 16777216 | tf_op jit(solution)/shard_map/slice | solution.py:24
  72.3 6.1 %fusion.79 = (bf16[2048,1024]{1,0:T(8,128)(2,1)}, bf16[2048,1024]{1,0:T(8,128)(2,1)}) fusion(bf16[2048,2048]{1,0:T(8,128)(2,1)} %bitcast.154), kind=kLoop, calls=%fused_computation.114 | loop fusion | bytes 16777216 | tf_op jit(solution)/shard_map/slice | solution.py:24
  79.1 1.3 copy.226
  80.4 6.5 %copy.215 = bf16[2048,1024]{0,1:T(8,128)(2,1)} copy(bf16[2048,1024]{1,0:T(8,128)(2,1)} %get-tuple-element.15) | data formatting | bytes 8388608 | tf_op jit(solution)/shard_map/slice | solution.py:24
  86.9 6.5 %copy.211 = bf16[2048,1024]{0,1:T(8,128)(2,1)} copy(bf16[2048,1024]{1,0:T(8,128)(2,1)} %get-tuple-element.16) | data formatting | bytes 8388608 | tf_op jit(solution)/shard_map/slice | solution.py:23
  93.4 7.5 %fusion.8 = (f32[128,4,2]{0,2,1:T(2,128)S(1)}, f32[4,2048,128,2]{2,1,3,0:T(8,128)}) fusion(pred[128,2048]{0,1:T(8,128)(4,1)S(1)} %compare_and_fusion, bf16[2048,4,256,1]{0,2,3,1:T(8,128)(2,1)} %bitcast.169, bf16[128,4,2,256]{0,3,2,1:T(8,128)(2,1)S(1)} %bitcast.157), kind=kOutput, calls=%fused_computation.17 | convolution fusion | flops 1080032256 | bytes 13373440 | tf_op jit(solution)/shard_map/rgjd,kgd->rgjk/dot_general | solution.py:25
  100.9 1.8 reshape_reshape.12
  102.7 9.7 %bitcast_reduce_fusion = (f32[256,4,2]{0,2,1:T(2,128)S(1)}, f32[4,256,2,2048]{3,1,2,0:T(8,128)}) fusion(pred[2048]{0:T(1024)(128)(4,1)S(1)} %add_compare_fusion, bf16[2048,4,256,1]{0,2,3,1:T(8,128)(2,1)} %bitcast.183, bf16[256,4,2,256]{3,2,1,0:T(2,128)(2,1)S(1)} %reshape_reshape.12), kind=kOutput, calls=%fused_computation.6 | convolution fusion | flops 2160064512 | bytes 22030336 | tf_op jit(solution)/shard_map/rgjd,kgd->rgjk/dot_general | solution.py:25
  112.5 0.7 reshape.332
  113.2 3.8 %all-to-all-start.1 = ((f32[8,1,256]{2,1,0:T(1,128)}), f32[8,1,256]{2,1,0:T(1,128)S(1)}, u32[]{:S(2)}, u32[]{:S(2)}) async-start(f32[8,1,256]{2,1,0:T(1,128)} %reshape.332), calls=%async_computation.1 | async-start | bytes 16384 | tf_op jit(solution)/shard_map/all_to_all | solution.py:164
  117.0 8.0 %fusion.2 = f32[256,4,2]{0,2,1:T(2,128)S(1)} fusion(f32[4,256,2,2048]{3,1,2,0:T(8,128)} %get-tuple-element.26, f32[256,4,2]{0,2,1:T(2,128)S(1)} %get-tuple-element.25, pred[2048]{0:T(1024)(128)(4,1)S(1)} %add_compare_fusion), kind=kLoop, calls=%fused_computation.10 | loop fusion | flops 20969472 | bytes 16795648 | tf_op jit(solution)/shard_map/reduce_sum | solution.py:35
  125.1 0.7 reshape.334
  125.8 4.2 %all-to-all-start.3 = ((f32[8,1,256]{2,1,0:T(1,128)}), f32[8,1,256]{2,1,0:T(1,128)S(1)}, u32[]{:S(2)}, u32[]{:S(2)}) async-start(f32[8,1,256]{2,1,0:T(1,128)} %reshape.334), calls=%async_computation.4 | async-start | bytes 16384 | tf_op jit(solution)/shard_map/all_to_all | solution.py:171
  130.0 8.9 %fusion.25 = f32[256,4,2,256]{3,0,2,1:T(8,128)S(1)} fusion(bf16[2048,4,256,1]{0,2,3,1:T(8,128)(2,1)} %bitcast.182, f32[4,256,2,2048]{3,1,2,0:T(8,128)} %get-tuple-element.26, f32[256,4,2]{0,2,1:T(2,128)S(1)} %get-tuple-element.25, pred[2048]{0:T(1024)(128)(4,1)S(1)} %add_compare_fusion), kind=kOutput, calls=%fused_computation.34 | convolution fusion | flops 2168455168 | bytes 23078912 | tf_op jit(solution)/shard_map/rgjk,kgd->rgjd/dot_general | solution.py:36
  138.9 1.6 copy.235
  140.5 2.7 %reshape_reshape.14 = f32[8,32,2048]{2,1,0:T(8,128)} reshape(f32[256,4,2,256]{3,2,1,0:T(2,128)S(1)} %copy.235) | data formatting | bytes 4194304 | tf_op jit(solution)/shard_map/reshape;reshape | solution.py:158
  143.2 4.2 %all-to-all-start.2 = ((f32[8,32,2048]{2,1,0:T(8,128)}), f32[8,32,2048]{2,1,0:T(8,128)S(1)}, u32[]{:S(2)}, u32[]{:S(2)}) async-start(f32[8,32,2048]{2,1,0:T(8,128)} %reshape_reshape.14), calls=%async_computation.2 | async-start | bytes 4194304 | tf_op jit(solution)/shard_map/all_to_all | solution.py:157
  147.4 8.4 %fusion.31 = f32[128,4,2,256]{3,0,2,1:T(8,128)} fusion(bf16[2048,4,256,1]{0,2,3,1:T(8,128)(2,1)} %bitcast.168, f32[4,2048,128,2]{2,1,3,0:T(8,128)} %get-tuple-element.30, f32[128,4,2]{0,2,1:T(2,128)S(1)} %get-tuple-element.29, pred[128,2048]{0,1:T(8,128)(4,1)S(1)} %compare_and_fusion), kind=kOutput, calls=%fused_computation.36 | convolution fusion | flops 1084227584 | bytes 13897728 | tf_op jit(solution)/shard_map/rgjk,kgd->rgjd/dot_general | solution.py:36
  155.8 2.6 %copy.218 = f32[128,4,2,256]{0,3,2,1:T(8,128)} copy(f32[128,4,2,256]{3,0,2,1:T(8,128)} %fusion.31) | data formatting | bytes 2097152 | tf_op jit(solution)/shard_map/rgjk,kgd->rgjd/transpose | solution.py:36
  158.4 2.5 %copy.220 = f32[128,2048]{1,0:T(8,128)} copy(f32[128,2048]{0,1:T(8,128)} %bitcast.171) | data formatting | bytes 2097152 | tf_op jit(solution)/shard_map/reshape | solution.py:45
  161.0 4.5 %fusion.9 = f32[128,4,2]{0,2,1:T(2,128)S(1)} fusion(f32[4,2048,128,2]{2,1,3,0:T(8,128)} %get-tuple-element.30, f32[128,4,2]{0,2,1:T(2,128)S(1)} %get-tuple-element.29, pred[128,2048]{0,1:T(8,128)(4,1)S(1)} %compare_and_fusion), kind=kLoop, calls=%fused_computation.18 | loop fusion | flops 10484736 | bytes 8658944 | tf_op jit(solution)/shard_map/reduce_sum | solution.py:35
  165.5 0.5 broadcast.193
  166.0 0.7 reduce.1
  166.7 0.7 reduce
  167.6 0.7 gather_fusion.3
  168.4 0.7 gather_fusion.1
  169.1 4.9 %all-to-all-done.2 = f32[8,32,2048]{2,1,0:T(8,128)S(1)} async-done(((f32[8,32,2048]{2,1,0:T(8,128)}), f32[8,32,2048]{2,1,0:T(8,128)S(1)}, u32[]{:S(2)}, u32[]{:S(2)}) %all-to-all-start.2) | async-done | bytes 2097184 | tf_op jit(solution)/shard_map/all_to_all | solution.py:157
  174.0 2.0 gather_fusion.2
  176.0 2.7 %fusion.81 = (bf16[1024,1024]{0,1:T(8,128)(2,1)S(1)}, bf16[1024,1024]{0,1:T(8,128)(2,1)S(1)}) fusion(bf16[1024,2048]{0,1:T(8,128)(2,1)} %all-gather.2.cloned.1.call-done), kind=kLoop, calls=%fused_computation.116 | loop fusion | bytes 8388608 | tf_op jit(solution)/shard_map/slice | solution.py:24
  178.7 1.0 bitcast_reduce_fusion.1
  179.7 0.7 fusion.19
  180.4 1.2 fusion.28
  182.3 12.1 %pmax.7 = f32[128,8]{0,1:T(8,128)S(1)} all-reduce(f32[128,8]{0,1:T(8,128)S(1)} %get-tuple-element.13), channel_id=1, replica_groups=mesh['row'=8,'col'=4] {'col'}, use_global_device_ids=true, to_apply=%region_9.10 | all-reduce | flops 1024 | bytes 8192 | tf_op jit(solution)/shard_map/pmax | solution.py:69
  195.5 0.3 copy.272
  199.3 0.3 copy.275
  200.6 2.5 %add_multiply_fusion = f32[128,2048]{1,0:T(8,128)} fusion(f32[128,2048]{1,0:T(8,128)S(1)} %bitcast.161, f32[128,2048]{1,0:T(8,128)S(1)} %copy-done, f32[128,2048]{1,0:T(8,128)S(1)} %bitcast.162, f32[128,2048]{1,0:T(8,128)S(1)} %bitcast.163, f32[128,2048]{1,0:T(8,128)S(1)} %copy-done.1, f32[128,2048]{1,0:T(8,128)S(1)} %bitcast.164, ...), kind=kLoop, calls=%fused_computation.42 | loop fusion | flops 3145728 | bytes 14680064 | tf_op jit(solution)/shard_map/mul | solution.py:72
  203.1 8.5 %psum.7 = f32[128,8]{0,1:T(8,128)S(1)} all-reduce(f32[128,8]{0,1:T(8,128)S(1)} %get-tuple-element.5), channel_id=1, replica_groups=mesh['row'=8,'col'=4] {'col'}, use_global_device_ids=true, to_apply=%region_15.16 | all-reduce | flops 1024 | bytes 8192 | tf_op jit(solution)/shard_map/psum | solution.py:74
  211.9 14.9 %reduce-scatter.2.cloned.1.call-done = f32[128,512]{1,0:T(8,128)} async-done(((f32[128,2048]{1,0:T(8,128)}), f32[128,512]{1,0:T(8,128)}) %reduce-scatter.2.cloned.1.call-update) | async-done | bytes 262160 | tf_op jit(solution)/shard_map/reduce_scatter | solution.py:71
  226.9 1.6 divide_convert_fusion
  (88 shorter events, 9.0 us)
Async XLA Ops:
  26.4 6.8 %copy-start.3 = (bf16[128,2048]{1,0:T(8,128)(2,1)S(1)}, bf16[128,2048]{1,0:T(8,128)(2,1)}, u32[]{:S(2)}) copy-start(bf16[128,2048]{1,0:T(8,128)(2,1)} %param.13) | copy-start | bytes 1572868
  28.7 6.4 %copy-start.5 = (s32[1,128]{1,0:T(1,128)S(1)}, s32[1,128]{1,0:T(1,128)}, u32[]{:S(2)}) copy-start(s32[1,128]{1,0:T(1,128)} %param.11) | copy-start | bytes 1540
  28.7 6.5 %copy-start.6 = (s32[32]{0:T(128)S(1)}, s32[32]{0:T(128)}, u32[]{:S(2)}) copy-start(s32[32]{0:T(128)} %param.17) | copy-start | bytes 388
  28.7 8.2 %copy-start.4 = (bf16[128,512]{1,0:T(8,128)(2,1)S(1)}, bf16[128,512]{1,0:T(8,128)(2,1)}, u32[]{:S(2)}) copy-start(bf16[128,512]{1,0:T(8,128)(2,1)} %param.10) | copy-start | bytes 393220
  28.7 72.2 %all-to-all-start = ((bf16[8,32,2048]{2,1,0:T(8,128)(2,1)}), bf16[8,32,2048]{2,1,0:T(8,128)(2,1)}, u32[]{:S(2)}, u32[]{:S(2)}) async-start(bf16[8,32,2048]{2,1,0:T(8,128)(2,1)} %bitcast.30), calls=%async_computation | async-start | bytes 2097152 | tf_op jit(solution)/shard_map/all_to_all | solution.py:151
  33.1 142.9 %all-gather.2.cloned.1.call-start = ((), (), s32[]{:S(2)}) async-start(), calls=%async_computation.5 | async-start | bytes 4718592 | tf_op jit(solution)/shard_map/all_gather | solution.py:108
  113.2 12.6 %all-to-all-start.1 = ((f32[8,1,256]{2,1,0:T(1,128)}), f32[8,1,256]{2,1,0:T(1,128)S(1)}, u32[]{:S(2)}, u32[]{:S(2)}) async-start(f32[8,1,256]{2,1,0:T(1,128)} %reshape.332), calls=%async_computation.1 | async-start | bytes 16384 | tf_op jit(solution)/shard_map/all_to_all | solution.py:164
  125.8 17.4 %all-to-all-start.3 = ((f32[8,1,256]{2,1,0:T(1,128)}), f32[8,1,256]{2,1,0:T(1,128)S(1)}, u32[]{:S(2)}, u32[]{:S(2)}) async-start(f32[8,1,256]{2,1,0:T(1,128)} %reshape.334), calls=%async_computation.4 | async-start | bytes 16384 | tf_op jit(solution)/shard_map/all_to_all | solution.py:171
  143.2 30.8 %all-to-all-start.2 = ((f32[8,32,2048]{2,1,0:T(8,128)}), f32[8,32,2048]{2,1,0:T(8,128)S(1)}, u32[]{:S(2)}, u32[]{:S(2)}) async-start(f32[8,32,2048]{2,1,0:T(8,128)} %reshape_reshape.14), calls=%async_computation.2 | async-start | bytes 4194304 | tf_op jit(solution)/shard_map/all_to_all | solution.py:157
  147.4 79.5 %reduce-scatter.2.cloned.1.call-start = ((), (), s32[]{:S(2)}) async-start(), calls=%async_computation.6 | async-start | bytes 1310720 | tf_op jit(solution)/shard_map/reduce_scatter | solution.py:71
  198.8 1.5 copy-start
  198.8 1.5 copy-start.1
  198.8 1.8 copy-start.2
Sparse Core Ops, SparseCore 0:
  35.8 39.5 all-gather.1
  203.2 23.6 reduce-scatter.1
where the time goes:
time: 237 us; the launch traced here: 235 us
  local copies, waits for them, and re-layouts  70.5 us (30%)
  blocking collectives  54.9 us (23%)
  matrix products  37.1 us (16%)
  other arithmetic  21.7 us (9%)
  waiting for transfers between devices  19.9 us (8%)
  starting transfers between devices  16.6 us (7%)
  between operations  14.5 us (6%)
    slice x5, local copies, waits for them, and re-layouts, attend(): keys_values[:, key_width:].reshape(key_count, KV_HEADS, HEAD_DIM)  21.4 us
    dot_general x4, matrix products, attend(): jnp.einsum('rgjk,kgd->rgjd', weights.astype(jnp.bfloat16), value_heads, p...  18.8 us
    dot_general x4, matrix products, attend(): jnp.einsum('rgjd,kgd->rgjk', query_heads, key_heads, preferred_element_ty...  18.4 us
    unnamed x30, local copies, waits for them, and re-layouts  18.3 us
    all_gather x1, blocking collectives, on_device(): lax.all_gather(queries, 'col', axis=1, tiled=True)  17.6 us
    all_gather x1, blocking collectives, on_device(): lax.all_gather(suffix_cache, 'col', axis=1, tiled=True)  16.8 us
    reduce_scatter x1, waiting for transfers between devices, combine_columns(): lax.psum_scatter(summed * jnp.repeat(factors, HEAD_DIM, axis=1), 'col', s...  14.9 us
    reduce_sum x4, other arithmetic, attend(): totals = jnp.sum(weights, axis=-1)  13.3 us
  transfers between devices with their start and end apart: 6, of which 2 were waited for; matrix products, arithmetic and copies ran while one was open for 46% of the time, Pallas kernels for 0%

commit v1 on v0

--- a/solution.py
+++ b/solution.py
@@ -1,8 +1,11 @@
+import functools
 import math
 
 import jax
 import jax.numpy as jnp
 from jax import lax
+from jax.experimental import pallas as pl
+from jax.experimental.pallas import tpu as pltpu
 from jax.sharding import PartitionSpec as P
 
 HEADS = 8
@@ -185,6 +188,384 @@
     return output.astype(jnp.bfloat16)
 
 
+LOW = -1e29
+LOG2_SCALE = 1.0 / (math.sqrt(HEAD_DIM) * math.log(2.0))
+KEY_WIDTH = KV_HEADS * HEAD_DIM
+PAIR = HEADS // KV_HEADS * HEAD_DIM
+KEY_STEP = 1024
+NT = (((1,), (1,)), ((), ()))
+NN = (((1,), (0,)), ((), ()))
+
+
+def dot(a, b, dims=NN, precision=None):
+    return lax.dot_general(a, b, dims, precision=precision, preferred_element_type=jnp.float32)
+
+
+def state_of(query_rows, keys, values, mask):
+    scores = dot(query_rows, keys, NT) * LOG2_SCALE
+    if mask is not None:
+        scores = jnp.where(mask, scores, NEG)
+    highest = jnp.maximum(jnp.max(scores, axis=1, keepdims=True), LOW)
+    weights = jnp.exp2(scores - highest)
+    totals = jnp.sum(weights, axis=1, keepdims=True)
+    return highest, totals, dot(weights.astype(jnp.bfloat16), values)
+
+
+def join(first, second):
+    highest = jnp.maximum(first[0], second[0])
+    a, b = jnp.exp2(first[0] - highest), jnp.exp2(second[0] - highest)
+    return highest, first[1] * a + second[1] * b, first[2] * a + second[2] * b
+
+
+def stacked(pair):
+    return jnp.concatenate([pair[:, :HEAD_DIM], pair[:, HEAD_DIM:]], axis=0)
+
+
+def fused_kernel(
+    n_row, n_col, cap,
+    q_ref, suf_ref, leaf_of_ref, parent_ref, leaf_len_ref, branch_len_ref, root_ref, branch_ref, leaf_ref,
+    out_ref,
+    qg, sbuf, rootb, leafv, branchv, sendq, brq, bro, brs, ret, rets, lm, ll, lo, fo, fs, fin, fins,
+    load_sem, q_s, q_r, suf_s, suf_r, root_s, root_r, fwd_s, fwd_r, bq_s, bq_r, bo_s, bo_r, bs_s, bs_r,
+    f_s, f_r, fs_s, fs_r,
+):
+    row, col = lax.axis_index("row"), lax.axis_index("col")
+    tokens = q_ref.shape[0]
+    slots = n_row * cap
+    branch_keys, leaf_keys = branchv.shape[0], leafv.shape[0]
+    leaf_width = leaf_keys // LEAF_ROW
+
+    def copy_to(src, dst, s, r, **where):
+        return pltpu.make_async_remote_copy(
+            src_ref=src, dst_ref=dst, send_sem=s, recv_sem=r, device_id=where,
+            device_id_type=pl.DeviceIdType.MESH,
+        )
+
+    loads = []
+    for i, (src, dst) in enumerate(((leaf_ref, leafv), (branch_ref, branchv))):
+        step = dst.shape[0] // 2
+        for j in range(2):
+            part = pl.ds(j * step, step)
+            loads.append(pltpu.make_async_copy(src.at[part], dst.at[part], load_sem.at[2 * i + j]))
+    for load in loads:
+        load.start()
+
+    barrier = pltpu.get_barrier_semaphore()
+    for k in range(1, n_row):
+        pl.semaphore_signal(barrier, inc=1, device_id={"row": (row + k) % n_row},
+                            device_id_type=pl.DeviceIdType.MESH)
+    for k in range(1, n_col):
+        pl.semaphore_signal(barrier, inc=1, device_id={"col": (col + k) % n_col},
+                            device_id_type=pl.DeviceIdType.MESH)
+    pl.semaphore_wait(barrier, n_row + n_col - 2)
+
+    sent = []
+
+    def send(copy):
+        copy.start()
+        sent.append(copy)
+        return copy
+
+    q_copies = [
+        send(copy_to(q_ref, qg.at[col], q_s.at[k], q_r.at[k], col=(col + k) % n_col))
+        for k in range(1, n_col)
+    ]
+    mate = row + 1 - 2 * (row % 2)
+
+    def root_copy(i, peer):
+        return copy_to(root_ref, rootb.at[row], root_s.at[i], root_r.at[i], row=peer)
+
+    def flip(k):
+        bit = 2 ** k
+        return row + bit - 2 * bit * ((row // bit) % 2)
+
+    flips = (flip(1), flip(2), n_row - 2 + 2 * (row % 2) - row)
+    root_copies = [send(root_copy(0, mate)), send(root_copy(1, flips[0])), send(root_copy(2, flips[1]))]
+    first = 2 * (col % 2)
+    for h in range(2):
+        @pl.when(first + h != col)
+        def _():
+            copy_to(suf_ref.at[:, pl.ds(h * HEAD_DIM, HEAD_DIM)], sbuf.at[col // 2], suf_s.at[h],
+                    suf_r.at[col // 2], col=first + h).start()
+
+        @pl.when(first + h == col)
+        def _():
+            sbuf[col // 2] = suf_ref[:, h * HEAD_DIM:(h + 1) * HEAD_DIM]
+    qg[col] = q_ref[...]
+    rootb[row] = root_ref[...]
+
+    def eye(n):
+        return lax.broadcasted_iota(jnp.int32, (n, n), 0) == lax.broadcasted_iota(jnp.int32, (n, n), 1)
+
+    def to_column(values):
+        return jnp.sum(jnp.where(eye(values.shape[1]), values, 0.0), axis=1, keepdims=True)
+
+    def to_row(values):
+        return jnp.sum(jnp.where(eye(values.shape[0]), values, 0.0), axis=0, keepdims=True)
+
+    leaf_row = leaf_of_ref[...].astype(jnp.float32)
+    leaf_col = to_column(leaf_row)
+    parent_row = parent_ref[...].astype(jnp.float32)
+    leaf_iota = lax.broadcasted_iota(jnp.int32, (tokens, LEAF_ROW), 1).astype(jnp.float32)
+    node_col = jnp.sum(jnp.where(leaf_col == leaf_iota, parent_row, 0.0), axis=1, keepdims=True)
+    node_row = to_row(node_col)
+    above = lax.broadcasted_iota(jnp.int32, (tokens, tokens), 0)
+    along = lax.broadcasted_iota(jnp.int32, (tokens, tokens), 1)
+    earlier = jnp.where((node_col == node_row) & (along < above), 1.0, 0.0)
+    slot_col = node_col * cap + jnp.sum(earlier, axis=1, keepdims=True)
+    slot_row = to_row(slot_col)
+    spread = jnp.where(
+        lax.broadcasted_iota(jnp.int32, (slots, tokens), 0).astype(jnp.float32) == slot_row, 1.0, 0.0
+    ).astype(jnp.bfloat16)
+    collect = jnp.where(
+        lax.broadcasted_iota(jnp.int32, (tokens, slots), 1).astype(jnp.float32) == slot_col, 1.0, 0.0
+    )
+    len_col = to_column(leaf_len_ref[...].astype(jnp.float32))
+    key_at = lax.broadcasted_iota(jnp.int32, (1, leaf_keys), 1)
+    key_leaf = (key_at // leaf_width).astype(jnp.float32)
+    key_place = (col * leaf_width + key_at % leaf_width).astype(jnp.float32)
+    rows32 = lax.broadcasted_iota(jnp.int32, (LEAF_ROW, leaf_keys), 0).astype(jnp.float32)
+    key_len = jnp.sum(jnp.where(rows32 == key_leaf, len_col, 0.0), axis=0, keepdims=True)
+    key_leaf = jnp.where(key_place < key_len, key_leaf, -1.0)
+    leaf_col2 = jnp.concatenate([leaf_col, leaf_col], axis=0)
+
+    for copy in q_copies:
+        copy.wait_recv()
+    for g in range(n_col):
+        gathered = dot(spread, qg[g]).astype(jnp.bfloat16)
+        sendq[:, :, g * PAIR:(g + 1) * PAIR] = gathered.reshape(n_row, cap, PAIR)
+    bq_copies = []
+    for k in range(1, n_row):
+        peer = (row + k) % n_row
+        bq_copies.append(send(copy_to(sendq.at[peer], brq.at[row], bq_s.at[k], bq_r.at[k], row=peer)))
+    root_copies.append(send(root_copy(3, flips[2])))
+    brq[row] = sendq[row]
+
+    loads[0].wait()
+    loads[1].wait()
+
+    def leaf_level(g, carry):
+        rows = stacked(qg[g])
+        states = []
+        for at in range(0, leaf_keys, KEY_STEP):
+            keys = leafv[at:at + KEY_STEP, pl.ds(pl.multiple_of(g * HEAD_DIM, HEAD_DIM), HEAD_DIM)]
+            values = leafv[
+                at:at + KEY_STEP, pl.ds(pl.multiple_of(KEY_WIDTH + g * HEAD_DIM, HEAD_DIM), HEAD_DIM)
+            ]
+            states.append(state_of(rows, keys, values, leaf_col2 == key_leaf[:, at:at + KEY_STEP]))
+        lm[g], ll[g], lo[g] = join(*states)
+        return carry
+
+    lax.fori_loop(0, KV_HEADS, leaf_level, 0)
+
+    fwd_copies = []
+    for i in range(2):
+        root_copies[1 + i].wait_recv()
+        fwd_copies.append(send(copy_to(rootb.at[flips[i]], rootb.at[flips[i]], fwd_s.at[i],
+                                       fwd_r.at[i], row=mate)))
+
+    for copy in bq_copies:
+        copy.wait_recv()
+    loads[2].wait()
+    loads[3].wait()
+    brs[...] = jnp.zeros_like(brs)
+
+    def branch_out(g, k):
+        peer = (row + k) % n_row
+        return copy_to(bro.at[g, peer], ret.at[g, row], bo_s.at[g, k], bo_r.at[g, k], row=peer)
+
+    def branch_level(g, carry):
+        rows = stacked(brq[:, :, pl.ds(pl.multiple_of(g * PAIR, PAIR), PAIR)].reshape(slots, PAIR))
+        states = []
+        for at in range(0, branch_keys, KEY_STEP):
+            keys = branchv[at:at + KEY_STEP, pl.ds(pl.multiple_of(g * HEAD_DIM, HEAD_DIM), HEAD_DIM)]
+            values = branchv[
+                at:at + KEY_STEP, pl.ds(pl.multiple_of(KEY_WIDTH + g * HEAD_DIM, HEAD_DIM), HEAD_DIM)
+            ]
+            place = col * branch_keys + at + lax.broadcasted_iota(jnp.int32, (1, KEY_STEP), 1)
+            states.append(state_of(rows, keys, values, place < branch_len_ref[...]))
+        highest, totals, summed = join(*states)
+        lane = lax.broadcasted_iota(jnp.int32, (slots, 128), 1)
+        stat = brs[...].reshape(slots, 128)
+        for j in range(2):
+            stat = jnp.where(lane == 4 * g + j, highest[j * slots:(j + 1) * slots], stat)
+            stat = jnp.where(lane == 4 * g + 2 + j, totals[j * slots:(j + 1) * slots], stat)
+        brs[...] = stat.reshape(n_row, cap, 128)
+        summed = jnp.concatenate([summed[:slots], summed[slots:]], axis=1).astype(jnp.bfloat16)
+        bro[g] = summed.reshape(n_row, cap, PAIR)
+        for k in range(1, n_row):
+            branch_out(g, k).start()
+        return carry
+
+    lax.fori_loop(0, KV_HEADS, branch_level, 0)
+    bs_copies = []
+    for k in range(1, n_row):
+        peer = (row + k) % n_row
+        bs_copies.append(send(copy_to(brs.at[peer], rets.at[row], bs_s.at[k], bs_r.at[k], row=peer)))
+    rets[row] = brs[row]
+    for g in range(KV_HEADS):
+        ret[g, row] = bro[g, row]
+
+    root_copies[3].wait_recv()
+    fwd_copies.append(send(copy_to(rootb.at[flips[2]], rootb.at[flips[2]], fwd_s.at[2], fwd_r.at[2],
+                                   row=mate)))
+    root_copies[0].wait_recv()
+    for copy in fwd_copies:
+        copy.wait_recv()
+
+    def root_level(g, carry):
+        rows = stacked(qg[g])
+        keys = rootb[:, :, pl.ds(pl.multiple_of(g * HEAD_DIM, HEAD_DIM), HEAD_DIM)]
+        values = rootb[:, :, pl.ds(pl.multiple_of(KEY_WIDTH + g * HEAD_DIM, HEAD_DIM), HEAD_DIM)]
+        keys, values = keys.reshape(-1, HEAD_DIM), values.reshape(-1, HEAD_DIM)
+        lm[g], ll[g], lo[g] = join((lm[g], ll[g], lo[g]), state_of(rows, keys, values, None))
+        return carry
+
+    lax.fori_loop(0, KV_HEADS, root_level, 0)
+
+    for copy in bs_copies:
+        copy.wait_recv()
+    stats = dot(collect, rets[...].reshape(slots, 128), precision=lax.Precision.HIGHEST)
+    collect16 = collect.astype(jnp.bfloat16)
+    lane = lax.broadcasted_iota(jnp.int32, (tokens, 128), 1)
+
+    def pick(index):
+        return jnp.sum(jnp.where(lane == index, stats, 0.0), axis=1, keepdims=True)
+
+    def final_copies(g):
+        return (
+            copy_to(fo.at[g], fin.at[col], f_s.at[g], f_r.at[col], col=g),
+            copy_to(fs.at[g], fins.at[col], fs_s.at[g], fs_r.at[col], col=g),
+        )
+
+    for g in range(KV_HEADS):
+        for k in range(1, n_row):
+            branch_out(g, k).wait_recv()
+        back = dot(collect16, ret[g].reshape(slots, PAIR))
+        summed, lines = [], []
+        for j in range(2):
+            part = slice(j * tokens, (j + 1) * tokens)
+            state = join(
+                (lm[g, part], ll[g, part], lo[g, part]),
+                (pick(4 * g + j), pick(4 * g + 2 + j), back[:, j * HEAD_DIM:(j + 1) * HEAD_DIM]),
+            )
+            summed.append(state[2])
+            lines += [to_row(state[0]), to_row(state[1])]
+        fo[g] = jnp.concatenate(summed, axis=1).astype(jnp.bfloat16)
+        fs[g] = jnp.concatenate(lines + lines, axis=0)
+
+        @pl.when(col != g)
+        def _():
+            for copy in final_copies(g):
+                copy.start()
+
+    for i, local in ((0, 0), (1, n_col - 1)):
+        @pl.when(col != local)
+        def _():
+            copy_to(suf_ref.at[:, pl.ds(0, HEAD_DIM)], sbuf.at[i], suf_s.at[0], suf_r.at[i],
+                    col=(col + 1) % n_col).wait_recv()
+    mask = (leaf_col2 == leaf_row) & (
+        lax.broadcasted_iota(jnp.int32, (2 * tokens, tokens), 1)
+        <= lax.broadcasted_iota(jnp.int32, (2 * tokens, tokens), 0) % tokens
+    )
+    state = state_of(stacked(q_ref[...]), sbuf[0], sbuf[1], mask)
+    fin[col] = fo[col]
+    fins[col] = fs[col]
+    for g in range(n_col):
+        @pl.when(col != g)
+        def _():
+            peer = g
+            copy_to(fo.at[g], fin.at[peer], f_s.at[g], f_r.at[peer], col=g).wait_recv()
+            copy_to(fs.at[g], fins.at[peer], fs_s.at[g], fs_r.at[peer], col=g).wait_recv()
+    for j in range(2):
+        part = slice(j * tokens, (j + 1) * tokens)
+        mine = tuple(entry[part] for entry in state)
+        for g in range(n_col):
+            lines = fins[g]
+            mine = join(mine, (
+                to_column(lines[2 * j:2 * j + 1]), to_column(lines[2 * j + 1:2 * j + 2]),
+                fin[g, :, j * HEAD_DIM:(j + 1) * HEAD_DIM].astype(jnp.float32),
+            ))
+        out_ref[:, j * HEAD_DIM:(j + 1) * HEAD_DIM] = (mine[2] / mine[1]).astype(out_ref.dtype)
+
+    for copy in sent:
+        copy.wait_send()
+    for h in range(2):
+        @pl.when(first + h != col)
+        def _():
+            copy_to(suf_ref.at[:, pl.ds(h * HEAD_DIM, HEAD_DIM)], sbuf.at[col // 2], suf_s.at[h],
+                    suf_r.at[col // 2], col=first + h).wait_send()
+    for g in range(KV_HEADS):
+        for k in range(1, n_row):
+            branch_out(g, k).wait_send()
+
+        @pl.when(col != g)
+        def _():
+            for copy in final_copies(g):
+                copy.wait_send()
+
+
+def on_device_fused(
+    queries, suffix_cache, suffix_leaf, leaf_parent, root_cache, branch_cache, branch_length, leaf_cache,
+    leaf_length,
+):
+    n_row, n_col = lax.axis_size("row"), lax.axis_size("col")
+    tokens = queries.shape[0]
+    cap = tokens // 16 * (LEAF_ROW // n_row)
+    slots = n_row * cap
+    width = branch_cache.shape[2]
+    branch = branch_cache.reshape(-1, width)
+    leaf = leaf_cache.reshape(-1, width)
+    bf16, f32 = jnp.bfloat16, jnp.float32
+    dma = pltpu.SemaphoreType.DMA
+    vmem = pltpu.VMEM
+    scratch = [
+        vmem((n_col, tokens, PAIR), bf16),
+        vmem((2, tokens, HEAD_DIM), bf16),
+        vmem((n_row,) + root_cache.shape, bf16),
+        vmem(leaf.shape, bf16),
+        vmem(branch.shape, bf16),
+        vmem((n_row, cap, width), bf16),
+        vmem((n_row, cap, width), bf16),
+        vmem((KV_HEADS, n_row, cap, PAIR), bf16),
+        vmem((n_row, cap, 128), f32),
+        vmem((KV_HEADS, n_row, cap, PAIR), bf16),
+        vmem((n_row, cap, 128), f32),
+        vmem((KV_HEADS, 2 * tokens, 1), f32),
+        vmem((KV_HEADS, 2 * tokens, 1), f32),
+        vmem((KV_HEADS, 2 * tokens, HEAD_DIM), f32),
+        vmem((KV_HEADS, tokens, PAIR), bf16),
+        vmem((KV_HEADS, 8, tokens), f32),
+        vmem((n_col, tokens, PAIR), bf16),
+        vmem((n_col, 8, tokens), f32),
+        dma((4,)),
+        dma((n_col,)), dma((n_col,)),
+        dma((2,)), dma((2,)),
+        dma((4,)), dma((4,)),
+        dma((3,)), dma((3,)),
+        dma((n_row,)), dma((n_row,)),
+        dma((KV_HEADS, n_row)), dma((KV_HEADS, n_row)),
+        dma((n_row,)), dma((n_row,)),
+        dma((n_col,)), dma((n_col,)),
+        dma((n_col,)), dma((n_col,)),
+    ]
+    in_vmem = pl.BlockSpec(memory_space=pltpu.VMEM)
+    anywhere = pl.BlockSpec(memory_space=pl.ANY)
+    return pl.pallas_call(
+        functools.partial(fused_kernel, n_row, n_col, cap),
+        out_shape=jax.ShapeDtypeStruct(queries.shape, queries.dtype),
+        in_specs=[in_vmem] * 7 + [anywhere] * 2,
+        out_specs=in_vmem,
+        scratch_shapes=scratch,
+        compiler_params=pltpu.CompilerParams(
+            collective_id=0, has_side_effects=True, vmem_limit_bytes=56 * 2**20
+        ),
+    )(
+        queries, suffix_cache, suffix_leaf, leaf_parent, leaf_length.reshape(1, -1),
+        branch_length.reshape(1, 1), root_cache, branch, leaf,
+    )
+
+
 def solution(mesh):
     in_specs = (
         P("row", "col"),
@@ -198,6 +579,8 @@
         P("row"),
     )
     out_specs = P("row", "col")
+    sizes = dict(mesh.shape)
+    body = on_device_fused if (sizes["row"], sizes["col"]) == (8, 4) else on_device
     return jax.shard_map(
-        on_device, mesh=mesh, in_specs=in_specs, out_specs=out_specs, check_vma=False
-    )
+        body, mesh=mesh, in_specs=in_specs, out_specs=out_specs, check_vma=False
+    )

time: 237 us -> 73.1 us (0.31)
  the two profiles are of different devices: /device:TPU:0 before, /device:TPU:24 now
where the time goes in v1:
time: 73.1 us; the launch traced here: 73 us
  Pallas kernels  70.7 us (97%)
  local copies, waits for them, and re-layouts  1.57 us (2%)
    pallas_call x1, Pallas kernels, on_device_fused(): pl.pallas_call(functools.partial(fused_kernel, n_row, n_col, cap), out_sh...  70.7 us
    unnamed x1, local copies, waits for them, and re-layouts  1.57 us

profile of v1, /device:TPU:24, one launch (start us, length us, event | category | flops | bytes accessed | tf_op | source)
XLA Modules:
  0.0 73.0 jit_solution(11654421298262203232)
XLA Ops:
  0.7 70.7 %shard_map.91 = bf16[128,512]{1,0:T(8,128)(2,1)} custom-call(bf16[128,512]{1,0:T(8,128)(2,1)} %q_ref.1, bf16[128,512]{1,0:T(8,128)(2,1)} %suf_ref.1, s32[1,128]{1,0:T(1,128)} %leaf_of_ref.1, s32[1,32]{1,0:T(1,128)} %parent_ref.1, s32[1,32]{1,0:T(1,128)} %bitcast.7, s32[1,1]{1,0:T(1,128)} %bitcast.4.branch_len_ref, bf16[128,2048]{1,0:T(8,128)(2,1)} %root_ref.1, ...), custom_call_target="tpu_custom_call" | custom-call | tf_op jit(solution)/shard_map/pallas_call | solution.py:554
  71.4 1.6 %copy.12 = bf16[128,512]{1,0:T(8,128)(2,1)} copy(bf16[128,512]{1,0:T(8,128)(2,1)} %shard_map.91) | data formatting | bytes 262144

commit v2 on v1

--- a/solution.py
+++ b/solution.py
@@ -225,7 +225,7 @@
     n_row, n_col, cap,
     q_ref, suf_ref, leaf_of_ref, parent_ref, leaf_len_ref, branch_len_ref, root_ref, branch_ref, leaf_ref,
     out_ref,
-    qg, sbuf, rootb, leafv, branchv, sendq, brq, bro, brs, ret, rets, lm, ll, lo, fo, fs, fin, fins,
+    qg, sbuf, rootb, leafv, branchv, sendq, brq, bro, bst, ret, rst, lm, ll, lo, fo, fs, fin, fins,
     load_sem, q_s, q_r, suf_s, suf_r, root_s, root_r, fwd_s, fwd_r, bq_s, bq_r, bo_s, bo_r, bs_s, bs_r,
     f_s, f_r, fs_s, fs_r,
 ):
@@ -241,6 +241,15 @@
             device_id_type=pl.DeviceIdType.MESH,
         )
 
+    def group(i):
+        return (col + i) % 2 + 2 * ((col // 2 + i // 2) % 2)
+
+    def head_lanes(i):
+        return pl.ds(pl.multiple_of(group(i) * HEAD_DIM, HEAD_DIM), HEAD_DIM)
+
+    def value_lanes(i):
+        return pl.ds(pl.multiple_of(KEY_WIDTH + group(i) * HEAD_DIM, HEAD_DIM), HEAD_DIM)
+
     loads = []
     for i, (src, dst) in enumerate(((leaf_ref, leafv), (branch_ref, branchv))):
         step = dst.shape[0] // 2
@@ -257,42 +266,6 @@
     for k in range(1, n_col):
         pl.semaphore_signal(barrier, inc=1, device_id={"col": (col + k) % n_col},
                             device_id_type=pl.DeviceIdType.MESH)
-    pl.semaphore_wait(barrier, n_row + n_col - 2)
-
-    sent = []
-
-    def send(copy):
-        copy.start()
-        sent.append(copy)
-        return copy
-
-    q_copies = [
-        send(copy_to(q_ref, qg.at[col], q_s.at[k], q_r.at[k], col=(col + k) % n_col))
-        for k in range(1, n_col)
-    ]
-    mate = row + 1 - 2 * (row % 2)
-
-    def root_copy(i, peer):
-        return copy_to(root_ref, rootb.at[row], root_s.at[i], root_r.at[i], row=peer)
-
-    def flip(k):
-        bit = 2 ** k
-        return row + bit - 2 * bit * ((row // bit) % 2)
-
-    flips = (flip(1), flip(2), n_row - 2 + 2 * (row % 2) - row)
-    root_copies = [send(root_copy(0, mate)), send(root_copy(1, flips[0])), send(root_copy(2, flips[1]))]
-    first = 2 * (col % 2)
-    for h in range(2):
-        @pl.when(first + h != col)
-        def _():
-            copy_to(suf_ref.at[:, pl.ds(h * HEAD_DIM, HEAD_DIM)], sbuf.at[col // 2], suf_s.at[h],
-                    suf_r.at[col // 2], col=first + h).start()
-
-        @pl.when(first + h == col)
-        def _():
-            sbuf[col // 2] = suf_ref[:, h * HEAD_DIM:(h + 1) * HEAD_DIM]
-    qg[col] = q_ref[...]
-    rootb[row] = root_ref[...]
 
     def eye(n):
         return lax.broadcasted_iota(jnp.int32, (n, n), 0) == lax.broadcasted_iota(jnp.int32, (n, n), 1)
@@ -312,14 +285,67 @@
     above = lax.broadcasted_iota(jnp.int32, (tokens, tokens), 0)
     along = lax.broadcasted_iota(jnp.int32, (tokens, tokens), 1)
     earlier = jnp.where((node_col == node_row) & (along < above), 1.0, 0.0)
-    slot_col = node_col * cap + jnp.sum(earlier, axis=1, keepdims=True)
-    slot_row = to_row(slot_col)
+    rank_col = jnp.sum(earlier, axis=1, keepdims=True)
+    slot_row = to_row(node_col * cap + rank_col)
     spread = jnp.where(
         lax.broadcasted_iota(jnp.int32, (slots, tokens), 0).astype(jnp.float32) == slot_row, 1.0, 0.0
     ).astype(jnp.bfloat16)
-    collect = jnp.where(
-        lax.broadcasted_iota(jnp.int32, (tokens, slots), 1).astype(jnp.float32) == slot_col, 1.0, 0.0
-    )
+
+    def spread_out(i, pair):
+        sendq[i] = dot(spread, pair).astype(jnp.bfloat16).reshape(n_row, cap, PAIR)
+
+    qg[0] = q_ref[...]
+    spread_out(0, q_ref[...])
+    pl.semaphore_wait(barrier, n_row + n_col - 2)
+
+    sent = []
+
+    def send(copy):
+        copy.start()
+        sent.append(copy)
+        return copy
+
+    def q_copy(i):
+        return copy_to(q_ref, qg.at[i], q_s.at[i], q_r.at[i], col=group(i))
+
+    def branch_query(i, k):
+        peer = (row + k) % n_row
+        return copy_to(sendq.at[i, peer], brq.at[i, row], bq_s.at[i, k], bq_r.at[i, k], row=peer)
+
+    def branch_out(i, k):
+        peer = (row + k) % n_row
+        return (
+            copy_to(bro.at[i, peer], ret.at[i, row], bo_s.at[i, k], bo_r.at[i, k], row=peer),
+            copy_to(bst.at[i, peer], rst.at[i, row], bs_s.at[i, k], bs_r.at[i, k], row=peer),
+        )
+
+    for i in range(1, n_col):
+        send(q_copy(i))
+    for k in range(1, n_row):
+        branch_query(0, k).start()
+
+    def flip(bit):
+        return row + bit - 2 * bit * ((row // bit) % 2)
+
+    mate, beside, below = flip(1), flip(2), flip(4)
+    mate_copy = send(copy_to(root_ref, rootb.at[1], root_s.at[0], root_r.at[0], row=mate))
+    rootb[0] = root_ref[...]
+
+    first = 2 * (col % 2)
+
+    def suffix_copy(h):
+        return copy_to(suf_ref.at[:, pl.ds(h * HEAD_DIM, HEAD_DIM)], sbuf.at[col // 2], suf_s.at[h],
+                       suf_r.at[col // 2], col=first + h)
+
+    for h in range(2):
+        @pl.when(first + h != col)
+        def _():
+            suffix_copy(h).start()
+
+        @pl.when(first + h == col)
+        def _():
+            sbuf[col // 2] = suf_ref[:, h * HEAD_DIM:(h + 1) * HEAD_DIM]
+
     len_col = to_column(leaf_len_ref[...].astype(jnp.float32))
     key_at = lax.broadcasted_iota(jnp.int32, (1, leaf_keys), 1)
     key_leaf = (key_at // leaf_width).astype(jnp.float32)
@@ -329,135 +355,103 @@
     key_leaf = jnp.where(key_place < key_len, key_leaf, -1.0)
     leaf_col2 = jnp.concatenate([leaf_col, leaf_col], axis=0)
 
-    for copy in q_copies:
-        copy.wait_recv()
-    for g in range(n_col):
-        gathered = dot(spread, qg[g]).astype(jnp.bfloat16)
-        sendq[:, :, g * PAIR:(g + 1) * PAIR] = gathered.reshape(n_row, cap, PAIR)
-    bq_copies = []
-    for k in range(1, n_row):
-        peer = (row + k) % n_row
-        bq_copies.append(send(copy_to(sendq.at[peer], brq.at[row], bq_s.at[k], bq_r.at[k], row=peer)))
-    root_copies.append(send(root_copy(3, flips[2])))
-    brq[row] = sendq[row]
-
     loads[0].wait()
     loads[1].wait()
 
-    def leaf_level(g, carry):
-        rows = stacked(qg[g])
+    def leaf_level(i):
+        rows = stacked(qg[i])
         states = []
         for at in range(0, leaf_keys, KEY_STEP):
-            keys = leafv[at:at + KEY_STEP, pl.ds(pl.multiple_of(g * HEAD_DIM, HEAD_DIM), HEAD_DIM)]
-            values = leafv[
-                at:at + KEY_STEP, pl.ds(pl.multiple_of(KEY_WIDTH + g * HEAD_DIM, HEAD_DIM), HEAD_DIM)
-            ]
-            states.append(state_of(rows, keys, values, leaf_col2 == key_leaf[:, at:at + KEY_STEP]))
-        lm[g], ll[g], lo[g] = join(*states)
+            states.append(state_of(
+                rows, leafv[at:at + KEY_STEP, head_lanes(i)], leafv[at:at + KEY_STEP, value_lanes(i)],
+                leaf_col2 == key_leaf[:, at:at + KEY_STEP],
+            ))
+        lm[i], ll[i], lo[i] = join(*states)
+
+    def arrive(i, carry):
+        @pl.when(i > 0)
+        def _():
+            q_copy(i).wait_recv()
+            spread_out(i, qg[i])
+            for k in range(1, n_row):
+                branch_query(i, k).start()
+
+        leaf_level(i)
         return carry
 
-    lax.fori_loop(0, KV_HEADS, leaf_level, 0)
-
-    fwd_copies = []
-    for i in range(2):
-        root_copies[1 + i].wait_recv()
-        fwd_copies.append(send(copy_to(rootb.at[flips[i]], rootb.at[flips[i]], fwd_s.at[i],
-                                       fwd_r.at[i], row=mate)))
-
-    for copy in bq_copies:
-        copy.wait_recv()
+    lax.fori_loop(0, n_col, arrive, 0)
+    beside_copy = send(copy_to(root_ref, rootb.at[2], root_s.at[1], root_r.at[1], row=beside))
+    below_copy = send(copy_to(root_ref, rootb.at[4], root_s.at[2], root_r.at[2], row=below))
+    for i in range(n_col):
+        brq[i, row] = sendq[i, row]
+
     loads[2].wait()
     loads[3].wait()
-    brs[...] = jnp.zeros_like(brs)
-
-    def branch_out(g, k):
-        peer = (row + k) % n_row
-        return copy_to(bro.at[g, peer], ret.at[g, row], bo_s.at[g, k], bo_r.at[g, k], row=peer)
-
-    def branch_level(g, carry):
-        rows = stacked(brq[:, :, pl.ds(pl.multiple_of(g * PAIR, PAIR), PAIR)].reshape(slots, PAIR))
+    slot_at = lax.broadcasted_iota(jnp.int32, (n_row, cap, 128), 1)
+    lane_at = lax.broadcasted_iota(jnp.int32, (n_row, cap, 128), 2)
+
+    def branch_level(i, carry):
+        for k in range(1, n_row):
+            branch_query(i, k).wait_recv()
+        rows = stacked(brq[i].reshape(slots, PAIR))
         states = []
         for at in range(0, branch_keys, KEY_STEP):
-            keys = branchv[at:at + KEY_STEP, pl.ds(pl.multiple_of(g * HEAD_DIM, HEAD_DIM), HEAD_DIM)]
-            values = branchv[
-                at:at + KEY_STEP, pl.ds(pl.multiple_of(KEY_WIDTH + g * HEAD_DIM, HEAD_DIM), HEAD_DIM)
-            ]
             place = col * branch_keys + at + lax.broadcasted_iota(jnp.int32, (1, KEY_STEP), 1)
-            states.append(state_of(rows, keys, values, place < branch_len_ref[...]))
+            states.append(state_of(
+                rows, branchv[at:at + KEY_STEP, head_lanes(i)], branchv[at:at + KEY_STEP, value_lanes(i)],
+                place < branch_len_ref[...],
+            ))
         highest, totals, summed = join(*states)
-        lane = lax.broadcasted_iota(jnp.int32, (slots, 128), 1)
-        stat = brs[...].reshape(slots, 128)
         for j in range(2):
-            stat = jnp.where(lane == 4 * g + j, highest[j * slots:(j + 1) * slots], stat)
-            stat = jnp.where(lane == 4 * g + 2 + j, totals[j * slots:(j + 1) * slots], stat)
-        brs[...] = stat.reshape(n_row, cap, 128)
+            for at, column in ((j, highest), (2 + j, totals)):
+                column = jnp.broadcast_to(column[j * slots:(j + 1) * slots], (slots, 128))
+                line = jnp.sum(
+                    jnp.where(slot_at == lane_at, column.reshape(n_row, cap, 128), 0.0), axis=1, keepdims=True
+                )
+                bst[i, :, at:at + 1, :] = line
+                bst[i, :, at + 4:at + 5, :] = line
         summed = jnp.concatenate([summed[:slots], summed[slots:]], axis=1).astype(jnp.bfloat16)
-        bro[g] = summed.reshape(n_row, cap, PAIR)
+        bro[i] = summed.reshape(n_row, cap, PAIR)
         for k in range(1, n_row):
-            branch_out(g, k).start()
+            for copy in branch_out(i, k):
+                copy.start()
         return carry
 
-    lax.fori_loop(0, KV_HEADS, branch_level, 0)
-    bs_copies = []
-    for k in range(1, n_row):
-        peer = (row + k) % n_row
-        bs_copies.append(send(copy_to(brs.at[peer], rets.at[row], bs_s.at[k], bs_r.at[k], row=peer)))
-    rets[row] = brs[row]
-    for g in range(KV_HEADS):
-        ret[g, row] = bro[g, row]
-
-    root_copies[3].wait_recv()
-    fwd_copies.append(send(copy_to(rootb.at[flips[2]], rootb.at[flips[2]], fwd_s.at[2], fwd_r.at[2],
-                                   row=mate)))
-    root_copies[0].wait_recv()
-    for copy in fwd_copies:
+    lax.fori_loop(0, n_col, branch_level, 0)
+    for i in range(n_col):
+        ret[i, row] = bro[i, row]
+        rst[i, row] = bst[i, row]
+
+    half = root_ref.shape[0] // 2
+    beside_copy.wait_recv()
+    below_copy.wait_recv()
+    low_copy = send(copy_to(rootb.at[2, pl.ds(0, half)], rootb.at[6, pl.ds(0, half)], fwd_s.at[0],
+                            fwd_r.at[0], row=below))
+    high_copy = send(copy_to(rootb.at[4, pl.ds(half, half)], rootb.at[6, pl.ds(half, half)], fwd_s.at[1],
+                             fwd_r.at[1], row=beside))
+    shared = [
+        send(copy_to(rootb.at[2], rootb.at[3], fwd_s.at[2], fwd_r.at[2], row=mate)),
+        send(copy_to(rootb.at[4], rootb.at[5], fwd_s.at[3], fwd_r.at[3], row=mate)),
+    ]
+    mate_copy.wait_recv()
+    for copy in shared:
         copy.wait_recv()
 
-    def root_level(g, carry):
-        rows = stacked(qg[g])
-        keys = rootb[:, :, pl.ds(pl.multiple_of(g * HEAD_DIM, HEAD_DIM), HEAD_DIM)]
-        values = rootb[:, :, pl.ds(pl.multiple_of(KEY_WIDTH + g * HEAD_DIM, HEAD_DIM), HEAD_DIM)]
-        keys, values = keys.reshape(-1, HEAD_DIM), values.reshape(-1, HEAD_DIM)
-        lm[g], ll[g], lo[g] = join((lm[g], ll[g], lo[g]), state_of(rows, keys, values, None))
+    def root_level(i, blocks):
+        keys, values = rootb[blocks, :, head_lanes(i)], rootb[blocks, :, value_lanes(i)]
+        state = state_of(
+            stacked(qg[i]), keys.reshape(-1, HEAD_DIM), values.reshape(-1, HEAD_DIM), None
+        )
+        lm[i], ll[i], lo[i] = join((lm[i], ll[i], lo[i]), state)
+
+    def near_root(i, carry):
+        root_level(i, slice(0, 6))
         return carry
 
-    lax.fori_loop(0, KV_HEADS, root_level, 0)
-
-    for copy in bs_copies:
-        copy.wait_recv()
-    stats = dot(collect, rets[...].reshape(slots, 128), precision=lax.Precision.HIGHEST)
-    collect16 = collect.astype(jnp.bfloat16)
-    lane = lax.broadcasted_iota(jnp.int32, (tokens, 128), 1)
-
-    def pick(index):
-        return jnp.sum(jnp.where(lane == index, stats, 0.0), axis=1, keepdims=True)
-
-    def final_copies(g):
-        return (
-            copy_to(fo.at[g], fin.at[col], f_s.at[g], f_r.at[col], col=g),
-            copy_to(fs.at[g], fins.at[col], fs_s.at[g], fs_r.at[col], col=g),
-        )
-
-    for g in range(KV_HEADS):
-        for k in range(1, n_row):
-            branch_out(g, k).wait_recv()
-        back = dot(collect16, ret[g].reshape(slots, PAIR))
-        summed, lines = [], []
-        for j in range(2):
-            part = slice(j * tokens, (j + 1) * tokens)
-            state = join(
-                (lm[g, part], ll[g, part], lo[g, part]),
-                (pick(4 * g + j), pick(4 * g + 2 + j), back[:, j * HEAD_DIM:(j + 1) * HEAD_DIM]),
-            )
-            summed.append(state[2])
-            lines += [to_row(state[0]), to_row(state[1])]
-        fo[g] = jnp.concatenate(summed, axis=1).astype(jnp.bfloat16)
-        fs[g] = jnp.concatenate(lines + lines, axis=0)
-
-        @pl.when(col != g)
-        def _():
-            for copy in final_copies(g):
-                copy.start()
+    lax.fori_loop(0, n_col, near_root, 0)
+    low_copy.wait_recv()
+    high_copy.wait_recv()
+    last = send(copy_to(rootb.at[6], rootb.at[7], fwd_s.at[4], fwd_r.at[4], row=mate))
 
     for i, local in ((0, 0), (1, n_col - 1)):
         @pl.when(col != local)
@@ -468,24 +462,71 @@
         lax.broadcasted_iota(jnp.int32, (2 * tokens, tokens), 1)
         <= lax.broadcasted_iota(jnp.int32, (2 * tokens, tokens), 0) % tokens
     )
-    state = state_of(stacked(q_ref[...]), sbuf[0], sbuf[1], mask)
-    fin[col] = fo[col]
-    fins[col] = fs[col]
-    for g in range(n_col):
-        @pl.when(col != g)
+    own_state = state_of(stacked(q_ref[...]), sbuf[0], sbuf[1], mask)
+    lm[0], ll[0], lo[0] = join((lm[0], ll[0], lo[0]), own_state)
+
+    last.wait_recv()
+    collect = jnp.where(
+        lax.broadcasted_iota(jnp.int32, (tokens, slots), 1).astype(jnp.float32) == node_col * cap + rank_col,
+        1.0, 0.0,
+    ).astype(jnp.bfloat16)
+    rank_here = along.astype(jnp.float32) == rank_col
+
+    def final_copies(i):
+        return (
+            copy_to(fo.at[i], fin.at[i], f_s.at[i], f_r.at[i], col=group(i)),
+            copy_to(fs.at[i], fins.at[i], fs_s.at[i], fs_r.at[i], col=group(i)),
+        )
+
+    def come_back(step, carry):
+        i = (step + 1) % n_col
+        root_level(i, slice(6, 8))
+        for k in range(1, n_row):
+            for copy in branch_out(i, k):
+                copy.wait_recv()
+        back = dot(collect, ret[i].reshape(slots, PAIR))
+        stats = rst[i]
+
+        def pick(index):
+            found = jnp.zeros((tokens, 128), jnp.float32)
+            for n in range(n_row):
+                found = jnp.where(node_col == n, stats[n, index:index + 1, :], found)
+            return jnp.sum(jnp.where(rank_here, found, 0.0), axis=1, keepdims=True)
+
+        summed, lines = [], []
+        for j in range(2):
+            part = slice(j * tokens, (j + 1) * tokens)
+            state = join(
+                (lm[i, part], ll[i, part], lo[i, part]),
+                (pick(j), pick(2 + j), back[:, j * HEAD_DIM:(j + 1) * HEAD_DIM]),
+            )
+            summed.append(state[2])
+            lines += [to_row(state[0]), to_row(state[1])]
+        fo[i] = jnp.concatenate(summed, axis=1).astype(jnp.bfloat16)
+        fs[i] = jnp.concatenate(lines + lines, axis=0)
+
+        @pl.when(i > 0)
         def _():
-            peer = g
-            copy_to(fo.at[g], fin.at[peer], f_s.at[g], f_r.at[peer], col=g).wait_recv()
-            copy_to(fs.at[g], fins.at[peer], fs_s.at[g], fs_r.at[peer], col=g).wait_recv()
+            for copy in final_copies(i):
+                copy.start()
+
+        return carry
+
+    lax.fori_loop(0, n_col, come_back, 0)
+    fin[0] = fo[0]
+    fins[0] = fs[0]
+    for i in range(1, n_col):
+        for copy in final_copies(i):
+            copy.wait_recv()
     for j in range(2):
-        part = slice(j * tokens, (j + 1) * tokens)
-        mine = tuple(entry[part] for entry in state)
-        for g in range(n_col):
-            lines = fins[g]
-            mine = join(mine, (
+        mine = None
+        for i in range(n_col):
+            lines = fins[i]
+            other = (
                 to_column(lines[2 * j:2 * j + 1]), to_column(lines[2 * j + 1:2 * j + 2]),
-                fin[g, :, j * HEAD_DIM:(j + 1) * HEAD_DIM].astype(jnp.float32),
-            ))
+                fin[i, :, j * HEAD_DIM:(j + 1) * HEAD_DIM].astype(jnp.float32),
+            )
+            mine = other if mine is None else join(mine, other)
         out_ref[:, j * HEAD_DIM:(j + 1) * HEAD_DIM] = (mine[2] / mine[1]).astype(out_ref.dtype)
 
     for copy in sent:
@@ -493,16 +534,22 @@
     for h in range(2):
         @pl.when(first + h != col)
         def _():
-            copy_to(suf_ref.at[:, pl.ds(h * HEAD_DIM, HEAD_DIM)], sbuf.at[col // 2], suf_s.at[h],
-                    suf_r.at[col // 2], col=first + h).wait_send()
-    for g in range(KV_HEADS):
+            suffix_copy(h).wait_send()
+
+    def drain(i, carry):
         for k in range(1, n_row):
-            branch_out(g, k).wait_send()
-
-        @pl.when(col != g)
+            branch_query(i, k).wait_send()
+            for copy in branch_out(i, k):
+                copy.wait_send()
+
+        @pl.when(i > 0)
         def _():
-            for copy in final_copies(g):
+            for copy in final_copies(i):
                 copy.wait_send()
+
+        return carry
+
+    lax.fori_loop(0, n_col, drain, 0)
 
 
 def on_device_fused(
@@ -525,12 +572,12 @@
         vmem((n_row,) + root_cache.shape, bf16),
         vmem(leaf.shape, bf16),
         vmem(branch.shape, bf16),
-        vmem((n_row, cap, width), bf16),
-        vmem((n_row, cap, width), bf16),
-        vmem((KV_HEADS, n_row, cap, PAIR), bf16),
-        vmem((n_row, cap, 128), f32),
-        vmem((KV_HEADS, n_row, cap, PAIR), bf16),
-        vmem((n_row, cap, 128), f32),
+        vmem((n_col, n_row, cap, PAIR), bf16),
+        vmem((n_col, n_row, cap, PAIR), bf16),
+        vmem((n_col, n_row, cap, PAIR), bf16),
+        vmem((n_col, n_row, 8, 128), f32),
+        vmem((n_col, n_row, cap, PAIR), bf16),
+        vmem((n_col, n_row, 8, 128), f32),
         vmem((KV_HEADS, 2 * tokens, 1), f32),
         vmem((KV_HEADS, 2 * tokens, 1), f32),
         vmem((KV_HEADS, 2 * tokens, HEAD_DIM), f32),
@@ -541,11 +588,11 @@
         dma((4,)),
         dma((n_col,)), dma((n_col,)),
         dma((2,)), dma((2,)),
-        dma((4,)), dma((4,)),
         dma((3,)), dma((3,)),
-        dma((n_row,)), dma((n_row,)),
-        dma((KV_HEADS, n_row)), dma((KV_HEADS, n_row)),
-        dma((n_row,)), dma((n_row,)),
+        dma((5,)), dma((5,)),
+        dma((n_col, n_row)), dma((n_col, n_row)),
+        dma((n_col, n_row)), dma((n_col, n_row)),
+        dma((n_col, n_row)), dma((n_col, n_row)),
         dma((n_col,)), dma((n_col,)),
         dma((n_col,)), dma((n_col,)),
     ]

time: 73.1 us -> 73.9 us (1.011)
  the two profiles are of different devices: /device:TPU:24 before, /device:TPU:0 now
where the time goes in v2:
time: 73.9 us; the launch traced here: 72.7 us
  Pallas kernels  70.5 us (95%)
  local copies, waits for them, and re-layouts  1.57 us (2%)
    pallas_call x1, Pallas kernels, on_device_fused(): pl.pallas_call(functools.partial(fused_kernel, n_row, n_col, cap), out_sh...  70.5 us
    unnamed x1, local copies, waits for them, and re-layouts  1.57 us

profile of v2, /device:TPU:0, one launch (start us, length us, event | category | flops | bytes accessed | tf_op | source)
XLA Modules:
  0.0 72.7 jit_solution(14111524095691628014)
XLA Ops:
  0.7 70.5 %shard_map.91 = bf16[128,512]{1,0:T(8,128)(2,1)} custom-call(bf16[128,512]{1,0:T(8,128)(2,1)} %q_ref.1, bf16[128,512]{1,0:T(8,128)(2,1)} %suf_ref.1, s32[1,128]{1,0:T(1,128)} %leaf_of_ref.1, s32[1,32]{1,0:T(1,128)} %parent_ref.1, s32[1,32]{1,0:T(1,128)} %bitcast.7, s32[1,1]{1,0:T(1,128)} %bitcast.4.branch_len_ref, bf16[128,2048]{1,0:T(8,128)(2,1)} %root_ref.1, ...), custom_call_target="tpu_custom_call" | custom-call | tf_op jit(solution)/shard_map/pallas_call | solution.py:601
  71.1 1.6 %copy.12 = bf16[128,512]{1,0:T(8,128)(2,1)} copy(bf16[128,512]{1,0:T(8,128)(2,1)} %shard_map.91) | data formatting | bytes 262144

commit v3 on v2

--- a/solution.py
+++ b/solution.py
@@ -188,11 +188,12 @@
     return output.astype(jnp.bfloat16)
 
 
-LOW = -1e29
+LOW = -1e28
 LOG2_SCALE = 1.0 / (math.sqrt(HEAD_DIM) * math.log(2.0))
 KEY_WIDTH = KV_HEADS * HEAD_DIM
 PAIR = HEADS // KV_HEADS * HEAD_DIM
-KEY_STEP = 1024
+KEY_STEP = 256
+VALUE_STEP = 512
 NT = (((1,), (1,)), ((), ()))
 NN = (((1,), (0,)), ((), ()))
 
@@ -201,14 +202,34 @@
     return lax.dot_general(a, b, dims, precision=precision, preferred_element_type=jnp.float32)
 
 
-def state_of(query_rows, keys, values, mask):
-    scores = dot(query_rows, keys, NT) * LOG2_SCALE
-    if mask is not None:
-        scores = jnp.where(mask, scores, NEG)
-    highest = jnp.maximum(jnp.max(scores, axis=1, keepdims=True), LOW)
-    weights = jnp.exp2(scores - highest)
-    totals = jnp.sum(weights, axis=1, keepdims=True)
-    return highest, totals, dot(weights.astype(jnp.bfloat16), values)
+def fold_lanes(values, operation):
+    folded = values[:, :128]
+    for at in range(128, values.shape[1], 128):
+        folded = operation(folded, values[:, at:at + 128])
+    return folded
+
+
+def state_of(query_rows, keys, values, mask, count, held):
+    rows = query_rows.shape[0]
+    widest = None
+    for at in range(0, count, KEY_STEP):
+        span = min(KEY_STEP, count - at)
+        scores = dot(query_rows, keys(at, span), NT)
+        if mask is not None:
+            scores = jnp.where(mask(at, span), scores, NEG)
+        held[:rows, at:at + span] = scores
+        folded = fold_lanes(scores, jnp.maximum)
+        widest = folded if widest is None else jnp.maximum(widest, folded)
+    highest = jnp.maximum(jnp.max(widest, axis=1, keepdims=True) * LOG2_SCALE, LOW)
+    totals, summed = None, None
+    for at in range(0, count, VALUE_STEP):
+        span = min(VALUE_STEP, count - at)
+        weights = jnp.exp2(held[:rows, at:at + span] * LOG2_SCALE - highest)
+        folded = fold_lanes(weights, jnp.add)
+        totals = folded if totals is None else totals + folded
+        product = dot(weights.astype(jnp.bfloat16), values(at, span))
+        summed = product if summed is None else summed + product
+    return highest, jnp.sum(totals, axis=1, keepdims=True), summed
 
 
 def join(first, second):
@@ -225,7 +246,7 @@
     n_row, n_col, cap,
     q_ref, suf_ref, leaf_of_ref, parent_ref, leaf_len_ref, branch_len_ref, root_ref, branch_ref, leaf_ref,
     out_ref,
-    qg, sbuf, rootb, leafv, branchv, sendq, brq, bro, bst, ret, rst, lm, ll, lo, fo, fs, fin, fins,
+    qg, sbuf, rootb, leafv, branchv, sendq, brq, bro, bst, ret, rst, lm, ll, lo, fo, fs, fin, fins, held,
     load_sem, q_s, q_r, suf_s, suf_r, root_s, root_r, fwd_s, fwd_r, bq_s, bq_r, bo_s, bo_r, bs_s, bs_r,
     f_s, f_r, fs_s, fs_r,
 ):
@@ -360,13 +381,13 @@
 
     def leaf_level(i):
         rows = stacked(qg[i])
-        states = []
-        for at in range(0, leaf_keys, KEY_STEP):
-            states.append(state_of(
-                rows, leafv[at:at + KEY_STEP, head_lanes(i)], leafv[at:at + KEY_STEP, value_lanes(i)],
-                leaf_col2 == key_leaf[:, at:at + KEY_STEP],
-            ))
-        lm[i], ll[i], lo[i] = join(*states)
+        lm[i], ll[i], lo[i] = state_of(
+            rows,
+            lambda at, span: leafv[at:at + span, head_lanes(i)],
+            lambda at, span: leafv[at:at + span, value_lanes(i)],
+            lambda at, span: leaf_col2 == key_leaf[:, at:at + span],
+            leaf_keys, held,
+        )
 
     def arrive(i, carry):
         @pl.when(i > 0)
@@ -394,14 +415,17 @@
         for k in range(1, n_row):
             branch_query(i, k).wait_recv()
         rows = stacked(brq[i].reshape(slots, PAIR))
-        states = []
-        for at in range(0, branch_keys, KEY_STEP):
-            place = col * branch_keys + at + lax.broadcasted_iota(jnp.int32, (1, KEY_STEP), 1)
-            states.append(state_of(
-                rows, branchv[at:at + KEY_STEP, head_lanes(i)], branchv[at:at + KEY_STEP, value_lanes(i)],
-                place < branch_len_ref[...],
-            ))
-        highest, totals, summed = join(*states)
+
+        def usable(at, span):
+            place = col * branch_keys + at + lax.broadcasted_iota(jnp.int32, (1, span), 1)
+            return place < branch_len_ref[...]
+
+        highest, totals, summed = state_of(
+            rows,
+            lambda at, span: branchv[at:at + span, head_lanes(i)],
+            lambda at, span: branchv[at:at + span, value_lanes(i)],
+            usable, branch_keys, held,
+        )
         for j in range(2):
             for at, column in ((j, highest), (2 + j, totals)):
                 column = jnp.broadcast_to(column[j * slots:(j + 1) * slots], (slots, 128))
@@ -438,9 +462,17 @@
         copy.wait_recv()
 
     def root_level(i, blocks):
-        keys, values = rootb[blocks, :, head_lanes(i)], rootb[blocks, :, value_lanes(i)]
+        size = root_ref.shape[0]
+
+        def part(lanes):
+            def take(at, span):
+                chosen = slice(blocks.start + at // size, blocks.start + (at + span) // size)
+                return rootb[chosen, :, lanes].reshape(span, HEAD_DIM)
+            return take
+
         state = state_of(
-            stacked(qg[i]), keys.reshape(-1, HEAD_DIM), values.reshape(-1, HEAD_DIM), None
+            stacked(qg[i]), part(head_lanes(i)), part(value_lanes(i)), None,
+            (blocks.stop - blocks.start) * size, held,
         )
         lm[i], ll[i], lo[i] = join((lm[i], ll[i], lo[i]), state)
 
@@ -462,7 +494,10 @@
         lax.broadcasted_iota(jnp.int32, (2 * tokens, tokens), 1)
         <= lax.broadcasted_iota(jnp.int32, (2 * tokens, tokens), 0) % tokens
     )
-    own_state = state_of(stacked(q_ref[...]), sbuf[0], sbuf[1], mask)
+    own_state = state_of(
+        stacked(q_ref[...]), lambda at, span: sbuf[0], lambda at, span: sbuf[1], lambda at, span: mask,
+        tokens, held,
+    )
     lm[0], ll[0], lo[0] = join((lm[0], ll[0], lo[0]), own_state)
 
     last.wait_recv()
@@ -585,6 +620,7 @@
         vmem((KV_HEADS, 8, tokens), f32),
         vmem((n_col, tokens, PAIR), bf16),
         vmem((n_col, 8, tokens), f32),
+        vmem((max(2 * slots, 2 * tokens), max(branch.shape[0], leaf.shape[0])), f32),
         dma((4,)),
         dma((n_col,)), dma((n_col,)),
         dma((2,)), dma((2,)),

time: 73.9 us -> 74.1 us (level)
  no operation moved by 1% of the time
where the time goes in v3:
time: 74.1 us; the launch traced here: 72.7 us
  Pallas kernels  70.4 us (95%)
  local copies, waits for them, and re-layouts  1.57 us (2%)
    pallas_call x1, Pallas kernels, on_device_fused(): pl.pallas_call(functools.partial(fused_kernel, n_row, n_col, cap), out_sh...  70.4 us
    unnamed x1, local copies, waits for them, and re-layouts  1.57 us

profile of v3, /device:TPU:0, one launch (start us, length us, event | category | flops | bytes accessed | tf_op | source)
XLA Modules:
  0.0 72.7 jit_solution(3073673263835203835)
XLA Ops:
  0.7 70.4 %shard_map.91 = bf16[128,512]{1,0:T(8,128)(2,1)} custom-call(bf16[128,512]{1,0:T(8,128)(2,1)} %q_ref.1, bf16[128,512]{1,0:T(8,128)(2,1)} %suf_ref.1, s32[1,128]{1,0:T(1,128)} %leaf_of_ref.1, s32[1,32]{1,0:T(1,128)} %parent_ref.1, s32[1,32]{1,0:T(1,128)} %bitcast.7, s32[1,1]{1,0:T(1,128)} %bitcast.4.branch_len_ref, bf16[128,2048]{1,0:T(8,128)(2,1)} %root_ref.1, ...), custom_call_target="tpu_custom_call" | custom-call | tf_op jit(solution)/shard_map/pallas_call | solution.py:637
  71.1 1.6 %copy.12 = bf16[128,512]{1,0:T(8,128)(2,1)} copy(bf16[128,512]{1,0:T(8,128)(2,1)} %shard_map.91) | data formatting | bytes 262144

commit v4 on v3

--- a/solution.py
+++ b/solution.py
@@ -358,15 +358,6 @@
         return copy_to(suf_ref.at[:, pl.ds(h * HEAD_DIM, HEAD_DIM)], sbuf.at[col // 2], suf_s.at[h],
                        suf_r.at[col // 2], col=first + h)
 
-    for h in range(2):
-        @pl.when(first + h != col)
-        def _():
-            suffix_copy(h).start()
-
-        @pl.when(first + h == col)
-        def _():
-            sbuf[col // 2] = suf_ref[:, h * HEAD_DIM:(h + 1) * HEAD_DIM]
-
     len_col = to_column(leaf_len_ref[...].astype(jnp.float32))
     key_at = lax.broadcasted_iota(jnp.int32, (1, leaf_keys), 1)
     key_leaf = (key_at // leaf_width).astype(jnp.float32)
@@ -389,20 +380,30 @@
             leaf_keys, held,
         )
 
-    def arrive(i, carry):
-        @pl.when(i > 0)
-        def _():
-            q_copy(i).wait_recv()
-            spread_out(i, qg[i])
-            for k in range(1, n_row):
-                branch_query(i, k).start()
-
+    def arrive(i):
+        q_copy(i).wait_recv()
+        spread_out(i, qg[i])
+        for k in range(1, n_row):
+            branch_query(i, k).start()
+
+    def leaf_and_next(i, carry):
         leaf_level(i)
+        arrive(i + 1)
         return carry
 
-    lax.fori_loop(0, n_col, arrive, 0)
+    lax.fori_loop(0, n_col - 1, leaf_and_next, 0)
     beside_copy = send(copy_to(root_ref, rootb.at[2], root_s.at[1], root_r.at[1], row=beside))
     below_copy = send(copy_to(root_ref, rootb.at[4], root_s.at[2], root_r.at[2], row=below))
+    for h in range(2):
+        @pl.when(first + h != col)
+        def _():
+            suffix_copy(h).start()
+
+        @pl.when(first + h == col)
+        def _():
+            sbuf[col // 2] = suf_ref[:, h * HEAD_DIM:(h + 1) * HEAD_DIM]
+
+    leaf_level(n_col - 1)
     for i in range(n_col):
         brq[i, row] = sendq[i, row]
 
@@ -441,10 +442,7 @@
                 copy.start()
         return carry
 
-    lax.fori_loop(0, n_col, branch_level, 0)
-    for i in range(n_col):
-        ret[i, row] = bro[i, row]
-        rst[i, row] = bst[i, row]
+    lax.fori_loop(0, n_col - 1, branch_level, 0)
 
     half = root_ref.shape[0] // 2
     beside_copy.wait_recv()
@@ -457,6 +455,11 @@
         send(copy_to(rootb.at[2], rootb.at[3], fwd_s.at[2], fwd_r.at[2], row=mate)),
         send(copy_to(rootb.at[4], rootb.at[5], fwd_s.at[3], fwd_r.at[3], row=mate)),
     ]
+    branch_level(n_col - 1, 0)
+    for i in range(n_col):
+        ret[i, row] = bro[i, row]
+        rst[i, row] = bst[i, row]
+
     mate_copy.wait_recv()
     for copy in shared:
         copy.wait_recv()

time: 74.1 us -> 72.2 us (0.974)
  Pallas kernels: 70.4 us -> 68.7 us
    pallas_call x1, Pallas kernels: 70.4 us -> 68.7 us  [on_device_fused(): pl.pallas_call(functools.partial(fused_kernel, n_row, n_col, cap), out_sh...]
where the time goes in v4:
time: 72.2 us; the launch traced here: 70.9 us
  Pallas kernels  68.7 us (95%)
  local copies, waits for them, and re-layouts  1.57 us (2%)
    pallas_call x1, Pallas kernels, on_device_fused(): pl.pallas_call(functools.partial(fused_kernel, n_row, n_col, cap), out_sh...  68.7 us
    unnamed x1, local copies, waits for them, and re-layouts  1.57 us

profile of v4, /device:TPU:0, one launch (start us, length us, event | category | flops | bytes accessed | tf_op | source)
XLA Modules:
  0.0 70.9 jit_solution(13591528344188322904)
XLA Ops:
  0.7 68.7 %shard_map.91 = bf16[128,512]{1,0:T(8,128)(2,1)} custom-call(bf16[128,512]{1,0:T(8,128)(2,1)} %q_ref.1, bf16[128,512]{1,0:T(8,128)(2,1)} %suf_ref.1, s32[1,128]{1,0:T(1,128)} %leaf_of_ref.1, s32[1,32]{1,0:T(1,128)} %parent_ref.1, s32[1,32]{1,0:T(1,128)} %bitcast.7, s32[1,1]{1,0:T(1,128)} %bitcast.4.branch_len_ref, bf16[128,2048]{1,0:T(8,128)(2,1)} %root_ref.1, ...), custom_call_target="tpu_custom_call" | custom-call | tf_op jit(solution)/shard_map/pallas_call | solution.py:640
  69.4 1.6 %copy.12 = bf16[128,512]{1,0:T(8,128)(2,1)} copy(bf16[128,512]{1,0:T(8,128)(2,1)} %shard_map.91) | data formatting | bytes 262144

commit v5 on v4

--- a/solution.py
+++ b/solution.py
@@ -350,6 +350,8 @@
 
     mate, beside, below = flip(1), flip(2), flip(4)
     mate_copy = send(copy_to(root_ref, rootb.at[1], root_s.at[0], root_r.at[0], row=mate))
+    beside_copy = send(copy_to(root_ref, rootb.at[2], root_s.at[1], root_r.at[1], row=beside))
+    below_copy = send(copy_to(root_ref, rootb.at[4], root_s.at[2], root_r.at[2], row=below))
     rootb[0] = root_ref[...]
 
     first = 2 * (col % 2)
@@ -392,8 +394,17 @@
         return carry
 
     lax.fori_loop(0, n_col - 1, leaf_and_next, 0)
-    beside_copy = send(copy_to(root_ref, rootb.at[2], root_s.at[1], root_r.at[1], row=beside))
-    below_copy = send(copy_to(root_ref, rootb.at[4], root_s.at[2], root_r.at[2], row=below))
+    half = root_ref.shape[0] // 2
+    beside_copy.wait_recv()
+    below_copy.wait_recv()
+    low_copy = send(copy_to(rootb.at[2, pl.ds(0, half)], rootb.at[6, pl.ds(0, half)], fwd_s.at[0],
+                            fwd_r.at[0], row=below))
+    high_copy = send(copy_to(rootb.at[4, pl.ds(half, half)], rootb.at[6, pl.ds(half, half)], fwd_s.at[1],
+                             fwd_r.at[1], row=beside))
+    shared = [
+        send(copy_to(rootb.at[2], rootb.at[3], fwd_s.at[2], fwd_r.at[2], row=mate)),
+        send(copy_to(rootb.at[4], rootb.at[5], fwd_s.at[3], fwd_r.at[3], row=mate)),
+    ]
     for h in range(2):
         @pl.when(first + h != col)
         def _():
@@ -444,17 +455,9 @@
 
     lax.fori_loop(0, n_col - 1, branch_level, 0)
 
-    half = root_ref.shape[0] // 2
-    beside_copy.wait_recv()
-    below_copy.wait_recv()
-    low_copy = send(copy_to(rootb.at[2, pl.ds(0, half)], rootb.at[6, pl.ds(0, half)], fwd_s.at[0],
-                            fwd_r.at[0], row=below))
-    high_copy = send(copy_to(rootb.at[4, pl.ds(half, half)], rootb.at[6, pl.ds(half, half)], fwd_s.at[1],
-                             fwd_r.at[1], row=beside))
-    shared = [
-        send(copy_to(rootb.at[2], rootb.at[3], fwd_s.at[2], fwd_r.at[2], row=mate)),
-        send(copy_to(rootb.at[4], rootb.at[5], fwd_s.at[3], fwd_r.at[3], row=mate)),
-    ]
+    low_copy.wait_recv()
+    high_copy.wait_recv()
+    last = send(copy_to(rootb.at[6], rootb.at[7], fwd_s.at[4], fwd_r.at[4], row=mate))
     branch_level(n_col - 1, 0)
     for i in range(n_col):
         ret[i, row] = bro[i, row]
@@ -463,6 +466,7 @@
     mate_copy.wait_recv()
     for copy in shared:
         copy.wait_recv()
+    last.wait_recv()
 
     def root_level(i, blocks):
         size = root_ref.shape[0]
@@ -479,14 +483,11 @@
         )
         lm[i], ll[i], lo[i] = join((lm[i], ll[i], lo[i]), state)
 
-    def near_root(i, carry):
-        root_level(i, slice(0, 6))
+    def all_root(i, carry):
+        root_level(i, slice(0, n_row))
         return carry
 
-    lax.fori_loop(0, n_col, near_root, 0)
-    low_copy.wait_recv()
-    high_copy.wait_recv()
-    last = send(copy_to(rootb.at[6], rootb.at[7], fwd_s.at[4], fwd_r.at[4], row=mate))
+    lax.fori_loop(0, n_col, all_root, 0)
 
     for i, local in ((0, 0), (1, n_col - 1)):
         @pl.when(col != local)
@@ -503,7 +504,6 @@
     )
     lm[0], ll[0], lo[0] = join((lm[0], ll[0], lo[0]), own_state)
 
-    last.wait_recv()
     collect = jnp.where(
         lax.broadcasted_iota(jnp.int32, (tokens, slots), 1).astype(jnp.float32) == node_col * cap + rank_col,
         1.0, 0.0,
@@ -518,7 +518,6 @@
 
     def come_back(step, carry):
         i = (step + 1) % n_col
-        root_level(i, slice(6, 8))
         for k in range(1, n_row):
             for copy in branch_out(i, k):
                 copy.wait_recv()

time: 72.2 us -> 64.3 us (0.89)
  Pallas kernels: 68.7 us -> 61.2 us
    pallas_call x1, Pallas kernels: 68.7 us -> 61.2 us  [on_device_fused(): pl.pallas_call(functools.partial(fused_kernel, n_row, n_col, cap), out_sh...]
where the time goes in v5:
time: 64.3 us; the launch traced here: 63.5 us
  Pallas kernels  61.2 us (95%)
  local copies, waits for them, and re-layouts  1.57 us (2%)
  between operations  0.66 us (1%)
    pallas_call x1, Pallas kernels, on_device_fused(): pl.pallas_call(functools.partial(fused_kernel, n_row, n_col, cap), out_sh...  61.2 us
    unnamed x1, local copies, waits for them, and re-layouts  1.57 us

profile of v5, /device:TPU:0, one launch (start us, length us, event | category | flops | bytes accessed | tf_op | source)
XLA Modules:
  0.0 63.5 jit_solution(14297386974181603654)
XLA Ops:
  0.7 61.2 %shard_map.91 = bf16[128,512]{1,0:T(8,128)(2,1)} custom-call(bf16[128,512]{1,0:T(8,128)(2,1)} %q_ref.1, bf16[128,512]{1,0:T(8,128)(2,1)} %suf_ref.1, s32[1,128]{1,0:T(1,128)} %leaf_of_ref.1, s32[1,32]{1,0:T(1,128)} %parent_ref.1, s32[1,32]{1,0:T(1,128)} %bitcast.7, s32[1,1]{1,0:T(1,128)} %bitcast.4.branch_len_ref, bf16[128,2048]{1,0:T(8,128)(2,1)} %root_ref.1, ...), custom_call_target="tpu_custom_call" | custom-call | tf_op jit(solution)/shard_map/pallas_call | solution.py:639
  61.9 1.6 %copy.12 = bf16[128,512]{1,0:T(8,128)(2,1)} copy(bf16[128,512]{1,0:T(8,128)(2,1)} %shard_map.91) | data formatting | bytes 262144

commit v6 on v4

--- a/solution.py
+++ b/solution.py
@@ -350,6 +350,8 @@
 
     mate, beside, below = flip(1), flip(2), flip(4)
     mate_copy = send(copy_to(root_ref, rootb.at[1], root_s.at[0], root_r.at[0], row=mate))
+    beside_copy = send(copy_to(root_ref, rootb.at[2], root_s.at[1], root_r.at[1], row=beside))
+    below_copy = send(copy_to(root_ref, rootb.at[4], root_s.at[2], root_r.at[2], row=below))
     rootb[0] = root_ref[...]
 
     first = 2 * (col % 2)
@@ -369,6 +371,8 @@
 
     loads[0].wait()
     loads[1].wait()
+
+    brq[0, row] = sendq[0, row]
 
     def leaf_level(i):
         rows = stacked(qg[i])
@@ -385,27 +389,14 @@
         spread_out(i, qg[i])
         for k in range(1, n_row):
             branch_query(i, k).start()
+        brq[i, row] = sendq[i, row]
 
     def leaf_and_next(i, carry):
         leaf_level(i)
         arrive(i + 1)
         return carry
 
-    lax.fori_loop(0, n_col - 1, leaf_and_next, 0)
-    beside_copy = send(copy_to(root_ref, rootb.at[2], root_s.at[1], root_r.at[1], row=beside))
-    below_copy = send(copy_to(root_ref, rootb.at[4], root_s.at[2], root_r.at[2], row=below))
-    for h in range(2):
-        @pl.when(first + h != col)
-        def _():
-            suffix_copy(h).start()
-
-        @pl.when(first + h == col)
-        def _():
-            sbuf[col // 2] = suf_ref[:, h * HEAD_DIM:(h + 1) * HEAD_DIM]
-
-    leaf_level(n_col - 1)
-    for i in range(n_col):
-        brq[i, row] = sendq[i, row]
+    lax.fori_loop(0, n_col - 2, leaf_and_next, 0)
 
     loads[2].wait()
     loads[3].wait()
@@ -442,8 +433,8 @@
                 copy.start()
         return carry
 
-    lax.fori_loop(0, n_col - 1, branch_level, 0)
-
+    branch_level(0, 0)
+    arrive(n_col - 1)
     half = root_ref.shape[0] // 2
     beside_copy.wait_recv()
     below_copy.wait_recv()
@@ -455,6 +446,20 @@
         send(copy_to(rootb.at[2], rootb.at[3], fwd_s.at[2], fwd_r.at[2], row=mate)),
         send(copy_to(rootb.at[4], rootb.at[5], fwd_s.at[3], fwd_r.at[3], row=mate)),
     ]
+    for h in range(2):
+        @pl.when(first + h != col)
+        def _():
+            suffix_copy(h).start()
+
+        @pl.when(first + h == col)
+        def _():
+            sbuf[col // 2] = suf_ref[:, h * HEAD_DIM:(h + 1) * HEAD_DIM]
+
+    lax.fori_loop(1, n_col - 1, branch_level, 0)
+
+    low_copy.wait_recv()
+    high_copy.wait_recv()
+    last = send(copy_to(rootb.at[6], rootb.at[7], fwd_s.at[4], fwd_r.at[4], row=mate))
     branch_level(n_col - 1, 0)
     for i in range(n_col):
         ret[i, row] = bro[i, row]
@@ -463,6 +468,7 @@
     mate_copy.wait_recv()
     for copy in shared:
         copy.wait_recv()
+    last.wait_recv()
 
     def root_level(i, blocks):
         size = root_ref.shape[0]
@@ -478,15 +484,6 @@
             (blocks.stop - blocks.start) * size, held,
         )
         lm[i], ll[i], lo[i] = join((lm[i], ll[i], lo[i]), state)
-
-    def near_root(i, carry):
-        root_level(i, slice(0, 6))
-        return carry
-
-    lax.fori_loop(0, n_col, near_root, 0)
-    low_copy.wait_recv()
-    high_copy.wait_recv()
-    last = send(copy_to(rootb.at[6], rootb.at[7], fwd_s.at[4], fwd_r.at[4], row=mate))
 
     for i, local in ((0, 0), (1, n_col - 1)):
         @pl.when(col != local)
@@ -503,7 +500,6 @@
     )
     lm[0], ll[0], lo[0] = join((lm[0], ll[0], lo[0]), own_state)
 
-    last.wait_recv()
     collect = jnp.where(
         lax.broadcasted_iota(jnp.int32, (tokens, slots), 1).astype(jnp.float32) == node_col * cap + rank_col,
         1.0, 0.0,
@@ -518,7 +514,12 @@
 
     def come_back(step, carry):
         i = (step + 1) % n_col
-        root_level(i, slice(6, 8))
+
+        @pl.when(i >= n_col - 2)
+        def _():
+            leaf_level(i)
+
+        root_level(i, slice(0, n_row))
         for k in range(1, n_row):
             for copy in branch_out(i, k):
                 copy.wait_recv()

time: 72.2 us -> 65.8 us (0.911); the launches traced: 70.9 us -> 65.7 us
  Pallas kernels: 68.7 us -> 63.5 us
    pallas_call x1, Pallas kernels: 68.7 us -> 63.5 us  [on_device_fused(): pl.pallas_call(functools.partial(fused_kernel, n_row, n_col, cap), out_sh...]
where the time goes in v6:
time: 65.8 us; the launch traced here: 65.7 us
  Pallas kernels  63.5 us (97%)
  local copies, waits for them, and re-layouts  1.57 us (2%)
  between operations  0.66 us (1%)
    pallas_call x1, Pallas kernels, on_device_fused(): pl.pallas_call(functools.partial(fused_kernel, n_row, n_col, cap), out_sh...  63.5 us
    unnamed x1, local copies, waits for them, and re-layouts  1.57 us

profile of v6, /device:TPU:0, one launch (start us, length us, event | category | flops | bytes accessed | tf_op | source)
XLA Modules:
  0.0 65.7 jit_solution(4593416387772507858)
XLA Ops:
  0.7 63.5 %shard_map.91 = bf16[128,512]{1,0:T(8,128)(2,1)} custom-call(bf16[128,512]{1,0:T(8,128)(2,1)} %q_ref.1, bf16[128,512]{1,0:T(8,128)(2,1)} %suf_ref.1, s32[1,128]{1,0:T(1,128)} %leaf_of_ref.1, s32[1,32]{1,0:T(1,128)} %parent_ref.1, s32[1,32]{1,0:T(1,128)} %bitcast.7, s32[1,1]{1,0:T(1,128)} %bitcast.4.branch_len_ref, bf16[128,2048]{1,0:T(8,128)(2,1)} %root_ref.1, ...), custom_call_target="tpu_custom_call" | custom-call | tf_op jit(solution)/shard_map/pallas_call | solution.py:641
  64.1 1.6 %copy.12 = bf16[128,512]{1,0:T(8,128)(2,1)} copy(bf16[128,512]{1,0:T(8,128)(2,1)} %shard_map.91) | data formatting | bytes 262144
